TPU v7x, 32 devices: a whole 2x2x4 slice. The times are simulated.
32 devices in a mesh: dom: 16 (over z, x, core), cls: 2 (over y).
Axes of the slice: x: 2, y: 2, z: 4, core: 2. Of those that a mesh axis runs over, the one named last changes fastest.
Arguments:
- images: bfloat16 [128, 9216], P(('dom', 'cls')), may hold values from -64 to 64
- ctf: float32 [128, 64], P(('dom', 'cls')), may hold values from 0.2 to 1
- inv_noise: float32 [64], replicated, may hold values from 0.5 to 2
- classes: bfloat16 [400, 9216], P('cls'), may hold values from -0.25 to 0.25
- candidates: int32 [128, 2], P(('dom', 'cls')), may hold values from 0 to 399, as said below
Outputs:
- class_sums: float32 [9216, 400], P('dom', 'cls')
- weight_sums: float32 [400, 64], P('cls')
- evidence: float32 [128], P(('dom', 'cls'))
Inputs may be any that keep to these rules, and one draw needn't show every extreme that they name: `candidates`: each row names 2 different classes. Among the 4 particles of one device, at most 4 name a class of any one block b (classes b * 200 to (b + 1) * 200 - 1); for each index along dom, the 2 devices that share it have one common block that exactly 4 particles of each of them name.
All inputs are finite; a program needn't handle non-finite values.
Results may differ from a plain program's by a relative error of at most 0.0053.
Values may be sent and summed in bfloat16 or wider, within the bound.
A program may use at most 64 MiB of HBM per device.

v0:
```python
import math

import jax
import jax.numpy as jnp
from jax import lax
from jax.sharding import PartitionSpec as P

ANGLES = 72
ROTATIONS = 36
TOP_CAND = 2


NEGATIVE = -1e30


def combined_all(value, axis, join):
    pieces = jax.tree.map(lambda part: lax.all_gather(part, axis), value)
    head = jax.tree.map(lambda part: part[0], pieces)
    tail = jax.tree.map(lambda part: part[1:], pieces)
    subtotal, _ = lax.scan(lambda subtotal, section: (join(subtotal, section), None), head, tail)
    return subtotal


def combine_totals(earlier, later):
    highest = jnp.maximum(earlier[0], later[0])
    return (
        highest,
        earlier[1] * jnp.exp(earlier[0] - highest) + later[1] * jnp.exp(later[0] - highest),
    )


def shards(images, ctf, inv_noise, classes, candidates):
    cls_count = lax.axis_size("cls")
    my_index = lax.axis_index("cls")
    part_dev = images.shape[0]
    class_block = classes.shape[0]
    features = images.shape[1]
    cycles = ctf.shape[1]
    capacity = min(5 * part_dev * TOP_CAND // (2 * cls_count), part_dev)
    group_size = cls_count * part_dev
    shift = features // ANGLES * (ANGLES // ROTATIONS)
    turn_ids = jnp.arange(ROTATIONS, dtype=jnp.int32)
    ctf_noise = ctf * inv_noise[None, :]
    weighted = (images.astype(jnp.float32) * jnp.tile(ctf_noise, (1, features // cycles))).astype(
        jnp.bfloat16
    )
    quadratic = (ctf * ctf * inv_noise[None, :]).astype(jnp.bfloat16)
    everyone = lax.all_gather(candidates, "cls", axis=0, tiled=True)
    block_ids = jnp.arange(class_block, dtype=jnp.int32) + my_index * class_block
    cand_mask = jnp.any(everyone[:, :, None] == block_ids[None, None, :], axis=1).astype(
        jnp.float32
    )
    owner_ids = jnp.arange(cls_count, dtype=jnp.int32)
    routed = jnp.any(
        (everyone // class_block)[:, :, None] == owner_ids[None, None, :], axis=1
    ).astype(jnp.int32)
    by_source = routed.reshape(cls_count, part_dev, cls_count)
    slot_of = jnp.cumsum(by_source, axis=1) - by_source
    slot_ids = jnp.arange(capacity, dtype=jnp.int32)
    mine_routed = lax.dynamic_index_in_dim(by_source, my_index, 0, keepdims=False)
    mine_slot = lax.dynamic_index_in_dim(slot_of, my_index, 0, keepdims=False)
    packing = (mine_routed.T[:, None, :] == 1) & (
        mine_slot.T[:, None, :] == slot_ids[None, :, None]
    )
    packing = packing.reshape(cls_count * capacity, part_dev).astype(jnp.bfloat16)
    send_data = jnp.dot(packing, weighted, preferred_element_type=jnp.float32).astype(jnp.bfloat16)
    send_quad = jnp.dot(packing, quadratic, preferred_element_type=jnp.float32).astype(jnp.bfloat16)
    row_data, row_quad = (
        lax.all_to_all(send_data, "cls", split_axis=0, concat_axis=0, tiled=True),
        lax.all_to_all(send_quad, "cls", split_axis=0, concat_axis=0, tiled=True),
    )
    into_mine = lax.dynamic_index_in_dim(by_source, my_index, 2, keepdims=False)
    slot_mine = lax.dynamic_index_in_dim(slot_of, my_index, 2, keepdims=False)
    selected = (into_mine[:, None, :] == 1) & (slot_mine[:, None, :] == slot_ids[None, :, None])
    diagonal = jnp.eye(cls_count, dtype=jnp.float32)
    unpack = (selected.astype(jnp.float32)[:, :, None, :] * diagonal[:, None, :, None]).reshape(
        cls_count * capacity, group_size
    )
    row_mask = jnp.dot(unpack, cand_mask, precision=lax.Precision.HIGHEST)
    row_count = row_data.shape[0]
    energy = jnp.sum(
        jnp.square(classes.astype(jnp.float32)).reshape(class_block, features // cycles, cycles),
        axis=1,
    )
    quad_wide = row_quad.astype(jnp.float32)
    norm_term = jnp.dot(quad_wide, energy.T, precision=lax.Precision.HIGHEST)
    twin_classes = jnp.concatenate([classes, classes], axis=1)
    feat_block = math.gcd(features, 1152)

    def add_block(block_index, running):
        offset = block_index * feat_block
        rotated = jax.vmap(
            lambda rotation: lax.dynamic_slice_in_dim(
                twin_classes, offset - rotation * shift + features, feat_block, 1
            )
        )(turn_ids)
        section = lax.dynamic_slice_in_dim(row_data, offset, feat_block, 1)
        return running + lax.dot_general(
            section, rotated, (((1,), (2,)), ((), ())), preferred_element_type=jnp.float32
        )

    cross = lax.fori_loop(
        0,
        features // feat_block,
        add_block,
        jnp.zeros((row_count, ROTATIONS, class_block), jnp.float32),
    )
    logits = cross - 0.5 * norm_term[:, None, :]
    live = jnp.broadcast_to(row_mask[:, None, :] > 0.5, logits.shape)
    masked = jnp.where(live, logits, NEGATIVE)
    peak = jnp.max(masked, axis=(1, 2))
    part_total = jnp.sum(jnp.where(live, jnp.exp(masked - peak[:, None, None]), 0.0), axis=(1, 2))
    group_peak = jnp.max(jnp.where(unpack > 0.5, peak[:, None], NEGATIVE), axis=0)
    group_total = jnp.sum(unpack * part_total[:, None], axis=0)
    top_all, total_all = combined_all((group_peak, group_total), "cls", combine_totals)
    group_evidence = top_all + jnp.log(total_all)
    own_evidence = lax.dynamic_slice_in_dim(group_evidence, my_index * part_dev, part_dev, 0)
    row_evidence = jnp.dot(unpack, group_evidence, precision=lax.Precision.HIGHEST)
    posterior = jnp.where(live, jnp.exp(logits - row_evidence[:, None, None]), 0.0).astype(
        jnp.bfloat16
    )
    weight_total = jnp.sum(posterior.astype(jnp.float32), axis=1)
    ctf_part = jnp.dot(weight_total.T, quad_wide, precision=lax.Precision.HIGHEST)
    weight_sums = lax.psum(ctf_part, "dom")
    twin_rows = jnp.concatenate([row_data, row_data], axis=1)

    def add_sums(block_index, running):
        offset = block_index * feat_block
        stacked = jax.vmap(
            lambda rotation: lax.dynamic_slice_in_dim(
                twin_rows, offset + rotation * shift, feat_block, 1
            )
        )(turn_ids)
        block_sum = lax.dot_general(
            posterior, stacked, (((0, 1), (1, 0)), ((), ())), preferred_element_type=jnp.float32
        )
        return lax.dynamic_update_slice_in_dim(running, block_sum, offset, 1)

    summed = lax.fori_loop(
        0, features // feat_block, add_sums, jnp.zeros((class_block, features), jnp.float32)
    )
    full_term = summed.T
    class_sums = lax.psum_scatter(full_term, "dom", scatter_dimension=0, tiled=True)
    return (class_sums, weight_sums, own_evidence)


def solution(mesh):
    in_specs = (
        P(("dom", "cls"), None),
        P(("dom", "cls"), None),
        P(),
        P("cls", None),
        P(("dom", "cls"), None),
    )
    out_specs = (P("dom", "cls"), P("cls", None), P(("dom", "cls")))
    return jax.shard_map(shards, mesh=mesh, in_specs=in_specs, out_specs=out_specs, check_vma=False)
```

profile of v0, /device:TPU:1, one launch (start us, length us, event | category | flops | bytes accessed | tf_op | source)
XLA Modules:
  0.0 1590.6 jit_solution(7118643023050376352)
XLA Ops:
  47.1 1004.8 %while.44 = (s32[]{:T(128)}, f32[8,36,200]{2,0,1:T(8,128)S(1)}, bf16[8,9216]{1,0:T(8,128)(2,1)S(1)}, bf16[200,18432]{1,0:T(8,128)(2,1)}, s32[]{:T(128)}, /*index=5*/s32[]{:T(128)}, s32[]{:T(128)}, s32[]{:T(128)}, s32[]{:T(128)}) while((s32[]{:T(128)}, f32[8,36,200]{2,0,1:T(8,128)S(1)}, bf16[8,9216]{1,0:T(8,128)(2,1)S(1)}, ...), condition=%wide.region_4.5_spmd.clone, body=%wide.region_3.4_spmd.clone.sunk | while | flops 132825824 | bytes 18056040 | solution.py:102
  47.2 117.2 %while.46 = (s32[]{:T(128)}, bf16[200,18432]{1,0:T(8,128)(2,1)}, s32[36,2]{0,1:T(2,128)S(1)}, bf16[36,200,1152]{2,1,0:T(8,128)(2,1)}, s32[]{:T(128)}) while((s32[]{:T(128)}, bf16[200,18432]{1,0:T(8,128)(2,1)}, s32[36,2]{0,1:T(2,128)S(1)}, bf16[36,200,1152]{2,1,0:T(8,128)(2,1)}, s32[]{:T(128)}) %tuple.109), condition=%wide.while_cond, body=%wide.while_body.sunk | while | flops 2 | bytes 922713 | solution.py:93
  172.8 117.2 %while.46 = (s32[]{:T(128)}, bf16[200,18432]{1,0:T(8,128)(2,1)}, s32[36,2]{0,1:T(2,128)S(1)}, bf16[36,200,1152]{2,1,0:T(8,128)(2,1)}, s32[]{:T(128)}) while((s32[]{:T(128)}, bf16[200,18432]{1,0:T(8,128)(2,1)}, s32[36,2]{0,1:T(2,128)S(1)}, bf16[36,200,1152]{2,1,0:T(8,128)(2,1)}, s32[]{:T(128)}) %tuple.109), condition=%wide.while_cond, body=%wide.while_body.sunk | while | flops 2 | bytes 922713 | solution.py:93
  298.4 117.2 %while.46 = (s32[]{:T(128)}, bf16[200,18432]{1,0:T(8,128)(2,1)}, s32[36,2]{0,1:T(2,128)S(1)}, bf16[36,200,1152]{2,1,0:T(8,128)(2,1)}, s32[]{:T(128)}) while((s32[]{:T(128)}, bf16[200,18432]{1,0:T(8,128)(2,1)}, s32[36,2]{0,1:T(2,128)S(1)}, bf16[36,200,1152]{2,1,0:T(8,128)(2,1)}, s32[]{:T(128)}) %tuple.109), condition=%wide.while_cond, body=%wide.while_body.sunk | while | flops 2 | bytes 922713 | solution.py:93
  424.0 117.2 %while.46 = (s32[]{:T(128)}, bf16[200,18432]{1,0:T(8,128)(2,1)}, s32[36,2]{0,1:T(2,128)S(1)}, bf16[36,200,1152]{2,1,0:T(8,128)(2,1)}, s32[]{:T(128)}) while((s32[]{:T(128)}, bf16[200,18432]{1,0:T(8,128)(2,1)}, s32[36,2]{0,1:T(2,128)S(1)}, bf16[36,200,1152]{2,1,0:T(8,128)(2,1)}, s32[]{:T(128)}) %tuple.109), condition=%wide.while_cond, body=%wide.while_body.sunk | while | flops 2 | bytes 922713 | solution.py:93
  541.2 8.3 convolution_add_fusion.2
  549.6 117.2 %while.46 = (s32[]{:T(128)}, bf16[200,18432]{1,0:T(8,128)(2,1)}, s32[36,2]{0,1:T(2,128)S(1)}, bf16[36,200,1152]{2,1,0:T(8,128)(2,1)}, s32[]{:T(128)}) while((s32[]{:T(128)}, bf16[200,18432]{1,0:T(8,128)(2,1)}, s32[36,2]{0,1:T(2,128)S(1)}, bf16[36,200,1152]{2,1,0:T(8,128)(2,1)}, s32[]{:T(128)}) %tuple.109), condition=%wide.while_cond, body=%wide.while_body.sunk | while | flops 2 | bytes 922713 | solution.py:93
  666.8 8.3 convolution_add_fusion.2
  675.2 117.2 %while.46 = (s32[]{:T(128)}, bf16[200,18432]{1,0:T(8,128)(2,1)}, s32[36,2]{0,1:T(2,128)S(1)}, bf16[36,200,1152]{2,1,0:T(8,128)(2,1)}, s32[]{:T(128)}) while((s32[]{:T(128)}, bf16[200,18432]{1,0:T(8,128)(2,1)}, s32[36,2]{0,1:T(2,128)S(1)}, bf16[36,200,1152]{2,1,0:T(8,128)(2,1)}, s32[]{:T(128)}) %tuple.109), condition=%wide.while_cond, body=%wide.while_body.sunk | while | flops 2 | bytes 922713 | solution.py:93
  792.5 8.3 convolution_add_fusion.2
  800.8 117.2 %while.46 = (s32[]{:T(128)}, bf16[200,18432]{1,0:T(8,128)(2,1)}, s32[36,2]{0,1:T(2,128)S(1)}, bf16[36,200,1152]{2,1,0:T(8,128)(2,1)}, s32[]{:T(128)}) while((s32[]{:T(128)}, bf16[200,18432]{1,0:T(8,128)(2,1)}, s32[36,2]{0,1:T(2,128)S(1)}, bf16[36,200,1152]{2,1,0:T(8,128)(2,1)}, s32[]{:T(128)}) %tuple.109), condition=%wide.while_cond, body=%wide.while_body.sunk | while | flops 2 | bytes 922713 | solution.py:93
  926.4 117.2 %while.46 = (s32[]{:T(128)}, bf16[200,18432]{1,0:T(8,128)(2,1)}, s32[36,2]{0,1:T(2,128)S(1)}, bf16[36,200,1152]{2,1,0:T(8,128)(2,1)}, s32[]{:T(128)}) while((s32[]{:T(128)}, bf16[200,18432]{1,0:T(8,128)(2,1)}, s32[36,2]{0,1:T(2,128)S(1)}, bf16[36,200,1152]{2,1,0:T(8,128)(2,1)}, s32[]{:T(128)}) %tuple.109), condition=%wide.while_cond, body=%wide.while_body.sunk | while | flops 2 | bytes 922713 | solution.py:93
  1063.0 392.9 %while.42 = (s32[]{:T(128)}, f32[200,9216]{1,0:T(8,128)}, bf16[8,18432]{1,0:T(8,128)(2,1)S(1)}, bf16[8,36,200]{2,0,1:T(8,128)(2,1)S(1)}, s32[]{:T(128)}, /*index=5*/s32[]{:T(128)}, s32[]{:T(128)}, s32[]{:T(128)}, s32[]{:T(128)}) while((s32[]{:T(128)}, f32[200,9216]{1,0:T(8,128)}, bf16[8,18432]{1,0:T(8,128)(2,1)S(1)}, ...), condition=%wide.region_11.12_spmd.clone, body=%wide.region_10.11_spmd.clone.sunk | while | flops 132710584 | bytes 1738088 | solution.py:139
  1063.1 47.6 %while.45 = (s32[]{:T(128)}, bf16[8,18432]{1,0:T(8,128)(2,1)S(1)}, s32[36,2]{0,1:T(2,128)S(1)}, bf16[36,8,1152]{2,1,0:T(8,128)(2,1)S(1)}, s32[]{:T(128)}) while((s32[]{:T(128)}, bf16[8,18432]{1,0:T(8,128)(2,1)S(1)}, s32[36,2]{0,1:T(2,128)S(1)}, bf16[36,8,1152]{2,1,0:T(8,128)(2,1)S(1)}, s32[]{:T(128)}) %tuple.112), condition=%wide.while_cond.1, body=%wide.while_body.1.sunk | while | flops 2 | bytes 36961 | solution.py:130
  1112.2 47.6 %while.45 = (s32[]{:T(128)}, bf16[8,18432]{1,0:T(8,128)(2,1)S(1)}, s32[36,2]{0,1:T(2,128)S(1)}, bf16[36,8,1152]{2,1,0:T(8,128)(2,1)S(1)}, s32[]{:T(128)}) while((s32[]{:T(128)}, bf16[8,18432]{1,0:T(8,128)(2,1)S(1)}, s32[36,2]{0,1:T(2,128)S(1)}, bf16[36,8,1152]{2,1,0:T(8,128)(2,1)S(1)}, s32[]{:T(128)}) %tuple.112), condition=%wide.while_cond.1, body=%wide.while_body.1.sunk | while | flops 2 | bytes 36961 | solution.py:130
  1161.3 47.6 %while.45 = (s32[]{:T(128)}, bf16[8,18432]{1,0:T(8,128)(2,1)S(1)}, s32[36,2]{0,1:T(2,128)S(1)}, bf16[36,8,1152]{2,1,0:T(8,128)(2,1)S(1)}, s32[]{:T(128)}) while((s32[]{:T(128)}, bf16[8,18432]{1,0:T(8,128)(2,1)S(1)}, s32[36,2]{0,1:T(2,128)S(1)}, bf16[36,8,1152]{2,1,0:T(8,128)(2,1)S(1)}, s32[]{:T(128)}) %tuple.112), condition=%wide.while_cond.1, body=%wide.while_body.1.sunk | while | flops 2 | bytes 36961 | solution.py:130
  1210.4 47.6 %while.45 = (s32[]{:T(128)}, bf16[8,18432]{1,0:T(8,128)(2,1)S(1)}, s32[36,2]{0,1:T(2,128)S(1)}, bf16[36,8,1152]{2,1,0:T(8,128)(2,1)S(1)}, s32[]{:T(128)}) while((s32[]{:T(128)}, bf16[8,18432]{1,0:T(8,128)(2,1)S(1)}, s32[36,2]{0,1:T(2,128)S(1)}, bf16[36,8,1152]{2,1,0:T(8,128)(2,1)S(1)}, s32[]{:T(128)}) %tuple.112), condition=%wide.while_cond.1, body=%wide.while_body.1.sunk | while | flops 2 | bytes 36961 | solution.py:130
  1259.5 47.6 %while.45 = (s32[]{:T(128)}, bf16[8,18432]{1,0:T(8,128)(2,1)S(1)}, s32[36,2]{0,1:T(2,128)S(1)}, bf16[36,8,1152]{2,1,0:T(8,128)(2,1)S(1)}, s32[]{:T(128)}) while((s32[]{:T(128)}, bf16[8,18432]{1,0:T(8,128)(2,1)S(1)}, s32[36,2]{0,1:T(2,128)S(1)}, bf16[36,8,1152]{2,1,0:T(8,128)(2,1)S(1)}, s32[]{:T(128)}) %tuple.112), condition=%wide.while_cond.1, body=%wide.while_body.1.sunk | while | flops 2 | bytes 36961 | solution.py:130
  1308.7 47.6 %while.45 = (s32[]{:T(128)}, bf16[8,18432]{1,0:T(8,128)(2,1)S(1)}, s32[36,2]{0,1:T(2,128)S(1)}, bf16[36,8,1152]{2,1,0:T(8,128)(2,1)S(1)}, s32[]{:T(128)}) while((s32[]{:T(128)}, bf16[8,18432]{1,0:T(8,128)(2,1)S(1)}, s32[36,2]{0,1:T(2,128)S(1)}, bf16[36,8,1152]{2,1,0:T(8,128)(2,1)S(1)}, s32[]{:T(128)}) %tuple.112), condition=%wide.while_cond.1, body=%wide.while_body.1.sunk | while | flops 2 | bytes 36961 | solution.py:130
  1357.8 47.6 %while.45 = (s32[]{:T(128)}, bf16[8,18432]{1,0:T(8,128)(2,1)S(1)}, s32[36,2]{0,1:T(2,128)S(1)}, bf16[36,8,1152]{2,1,0:T(8,128)(2,1)S(1)}, s32[]{:T(128)}) while((s32[]{:T(128)}, bf16[8,18432]{1,0:T(8,128)(2,1)S(1)}, s32[36,2]{0,1:T(2,128)S(1)}, bf16[36,8,1152]{2,1,0:T(8,128)(2,1)S(1)}, s32[]{:T(128)}) %tuple.112), condition=%wide.while_cond.1, body=%wide.while_body.1.sunk | while | flops 2 | bytes 36961 | solution.py:130
  1406.9 47.6 %while.45 = (s32[]{:T(128)}, bf16[8,18432]{1,0:T(8,128)(2,1)S(1)}, s32[36,2]{0,1:T(2,128)S(1)}, bf16[36,8,1152]{2,1,0:T(8,128)(2,1)S(1)}, s32[]{:T(128)}) while((s32[]{:T(128)}, bf16[8,18432]{1,0:T(8,128)(2,1)S(1)}, s32[36,2]{0,1:T(2,128)S(1)}, bf16[36,8,1152]{2,1,0:T(8,128)(2,1)S(1)}, s32[]{:T(128)}) %tuple.112), condition=%wide.while_cond.1, body=%wide.while_body.1.sunk | while | flops 2 | bytes 36961 | solution.py:130
  1455.9 9.0 copy.50
  1465.7 60.3 %psum.7 = f32[200,64]{0,1:T(8,128)} all-reduce(f32[200,64]{0,1:T(8,128)S(1)} %fusion.35), channel_id=1, replica_groups=mesh['dom'=16,'cls'=2] {'dom'}, use_global_device_ids=true, to_apply=%region_14.15 | all-reduce | flops 12800 | bytes 102400 | tf_op jit(solution)/shard_map/psum | solution.py:124
  1526.0 55.6 %reduce-scatter.4.cloned.1.call-done = f32[576,200]{1,0:T(8,128)} async-done(((f32[9216,200]{1,0:T(8,128)}), f32[576,200]{1,0:T(8,128)}) %reduce-scatter.4.cloned.1.call-update) | async-done | bytes 460816
  (1856 shorter events, 1425.2 us)
Async XLA Ops:
  13.3 26.9 %all-to-all-start.1 = ((bf16[2,2,128]{2,1,0:T(2,128)(2,1)}), bf16[2,2,128]{2,1,0:T(2,128)(2,1)S(1)}, u32[]{:S(2)}, u32[]{:S(2)}) async-start(bf16[2,2,128]{2,1,0:T(2,128)(2,1)} %reshape.221), calls=%async_computation.1 | async-start | bytes 2048 | tf_op jit(solution)/shard_map/all_to_all | solution.py:70
  23.5 7.0 copy-start
  30.5 4.4 copy-start.1
  40.2 6.8 all-to-all-start
  43.7 1538.0 %reduce-scatter.4.cloned.1.call-start = ((), (), s32[]{:S(2)}) async-start(), calls=%async_computation.3 | async-start | bytes 10027008
Sparse Core Ops, SparseCore 0:
  1465.0 116.5 reduce-scatter.3
where the time goes:
time: 1610 us; the launch traced here: 1590 us
  local copies, waits for them, and re-layouts  1340 us (83%)
  matrix products  79.8 us (5%)
  blocking collectives  70.4 us (4%)
  waiting for transfers between devices  58.8 us (4%)
  other arithmetic  17.4 us (1%)
    gather x1728, local copies, waits for them, and re-layouts  1320 us
    dot_general x8, matrix products, add_block(): lax.dot_general(section, rotated, (((1,), (2,)), ((), ())), preferred_ele...  66.5 us
    psum x1, blocking collectives, shards(): weight_sums = lax.psum(ctf_part, 'dom')  60.3 us
    unnamed x2, waiting for transfers between devices  55.6 us
  transfers between devices with their start and end apart: 3, of which 2 were waited for; matrix products, arithmetic and copies ran while one was open for 2% of the time, Pallas kernels for 0%

commit v1 on v0

--- a/solution.py
+++ b/solution.py
@@ -1,8 +1,11 @@
+import functools
 import math
 
 import jax
 import jax.numpy as jnp
 from jax import lax
+from jax.experimental import pallas as pl
+from jax.experimental.pallas import tpu as pltpu
 from jax.sharding import PartitionSpec as P
 
 ANGLES = 72
@@ -144,6 +147,337 @@
     return (class_sums, weight_sums, own_evidence)
 
 
+MESH = pl.DeviceIdType.MESH
+LANES = 128
+
+
+def estep_kernel(
+    doms,
+    images_ref,
+    ctf_ref,
+    noise_ref,
+    cand_ref,
+    classes_ref,
+    sums_ref,
+    weight_ref,
+    evidence_ref,
+    held,
+    own_wide,
+    own_send,
+    other_recv,
+    other_wide,
+    group_wide,
+    twin_even,
+    twin_odd,
+    framed,
+    part_send,
+    part_recv,
+    ids_send,
+    ids_recv,
+    stage,
+    arrived,
+    load_sem,
+    pair_send_sem,
+    pair_recv_sem,
+    ids_send_sem,
+    ids_recv_sem,
+    data_send_sem,
+    data_recv_sem,
+):
+    me = lax.axis_index("dom")
+    side = lax.axis_index("cls")
+    part_dev, features = images_ref.shape
+    cycles = ctf_ref.shape[1]
+    class_block = held.shape[0]
+    shift = framed.shape[1] // ROTATIONS
+    group = 2 * part_dev
+    rows = ROTATIONS * group
+    pairs = TOP_CAND * group
+    own_rows = ROTATIONS * part_dev
+    share = features // doms
+    wide = stage.shape[1]
+    peers = [lax.rem(me + step, doms) for step in range(1, doms)]
+
+    load = pltpu.make_async_copy(classes_ref, held, load_sem)
+    load.start()
+    barrier = pltpu.get_barrier_semaphore()
+    pl.semaphore_signal(barrier, inc=1, device_id={"cls": 1 - side}, device_id_type=MESH)
+    for peer in peers:
+        pl.semaphore_signal(barrier, inc=1, device_id={"dom": peer}, device_id_type=MESH)
+
+    ctf = ctf_ref[...]
+    noise = noise_ref[...]
+    factor = jnp.concatenate([ctf * noise] * (shift // cycles), axis=1)
+    quad = (ctf * ctf * noise).astype(jnp.bfloat16).astype(jnp.float32)
+    cand = cand_ref[...]
+
+    def local_ids(block, column):
+        local = cand[:, column : column + 1] - block * class_block
+        inside = (local >= 0) & (local < class_block)
+        local = jnp.where(inside, local, -1).astype(jnp.float32)
+        return jnp.broadcast_to(local, (part_dev, cycles))
+
+    def extras(block):
+        return jnp.concatenate([quad, quad, local_ids(block, 0), local_ids(block, 1)], axis=1)
+
+    for turn in range(ROTATIONS):
+        piece = images_ref[:, turn * shift : (turn + 1) * shift].astype(jnp.float32) * factor
+        piece = piece.astype(jnp.bfloat16).astype(jnp.float32)
+        own_wide[turn * part_dev : (turn + 1) * part_dev, :] = piece
+        group_wide[turn * group : turn * group + part_dev, :] = piece
+    own_wide[own_rows : own_rows + 16, :] = jnp.zeros((16, shift), jnp.float32)
+    own_wide[own_rows : own_rows + part_dev, :] = extras(1 - side)
+    own_send[...] = own_wide[...].astype(jnp.bfloat16)
+
+    pl.semaphore_wait(barrier, doms)
+    swap = pltpu.make_async_remote_copy(
+        src_ref=own_send,
+        dst_ref=other_recv,
+        send_sem=pair_send_sem.at[0],
+        recv_sem=pair_recv_sem.at[0],
+        device_id={"cls": 1 - side},
+        device_id_type=MESH,
+    )
+    swap.start()
+
+    load.wait()
+    energy = jnp.zeros((class_block, LANES), jnp.float32)
+    for start in range(0, features, LANES):
+        part = held[:, start : start + LANES].astype(jnp.float32)
+        energy = energy + part * part
+
+    swap.wait()
+    other_wide[...] = other_recv[...].astype(jnp.float32)
+    for turn in range(ROTATIONS):
+        group_wide[turn * group + part_dev : (turn + 1) * group, :] = other_wide[
+            turn * part_dev : (turn + 1) * part_dev, :
+        ]
+    info = jnp.concatenate([extras(side), other_wide[own_rows : own_rows + part_dev, :]], axis=0)
+    quad_group = info[:, :LANES]
+    first_id = info[:, 2 * cycles : 2 * cycles + 1]
+    second_id = info[:, 3 * cycles : 3 * cycles + 1]
+
+    ids_send[...] = jnp.broadcast_to(
+        jnp.concatenate([first_id, second_id], axis=0), (pairs, LANES)
+    ).astype(jnp.bfloat16)
+    mine = pl.ds(pl.multiple_of(me * pairs, pairs), pairs)
+    ids_recv[mine, :] = ids_send[...]
+    id_copies = []
+    for step, peer in enumerate(peers):
+        copy = pltpu.make_async_remote_copy(
+            src_ref=ids_send,
+            dst_ref=ids_recv.at[mine, :],
+            send_sem=ids_send_sem.at[step],
+            recv_sem=ids_recv_sem.at[step],
+            device_id={"dom": peer},
+            device_id_type=MESH,
+        )
+        copy.start()
+        id_copies.append(copy)
+
+    even = group_wide[...].astype(jnp.bfloat16)
+    odd = jnp.concatenate([group_wide[group:, :], group_wide[:group, :]], axis=0).astype(
+        jnp.bfloat16
+    )
+    twin_even[:rows, :] = even
+    twin_even[rows:, :] = even
+    twin_odd[:rows, :] = odd
+    twin_odd[rows:, :] = odd
+    for turn in range(ROTATIONS):
+        window = twin_odd if turn % 2 else twin_even
+        begin = (turn - turn % 2) * group
+        framed[:, turn * shift : (turn + 1) * shift] = window[begin : begin + rows, :]
+
+    contract_last = (((1,), (1,)), ((), ()))
+    cross = lax.dot_general(
+        held[...], framed[...], contract_last, preferred_element_type=jnp.float32
+    )
+    norm = lax.dot_general(
+        energy,
+        jnp.concatenate([quad_group] * ROTATIONS, axis=0),
+        contract_last,
+        precision=lax.Precision.HIGHEST,
+        preferred_element_type=jnp.float32,
+    )
+    logits = cross - 0.5 * norm
+
+    lane = lax.broadcasted_iota(jnp.int32, (group, rows), 1)
+    own_lane = (lane & (group - 1)) == lax.broadcasted_iota(jnp.int32, (group, rows), 0)
+    class_row = lax.broadcasted_iota(jnp.int32, (class_block, rows), 0).astype(jnp.float32)
+
+    def pick(ids):
+        wanted = jnp.sum(jnp.where(own_lane, ids, 0.0), axis=0, keepdims=True)
+        value = jnp.sum(jnp.where(class_row == wanted, logits, 0.0), axis=0, keepdims=True)
+        live = own_lane & (ids >= 0.0)
+        return live, jnp.broadcast_to(value, (group, rows))
+
+    live_a, value_a = pick(first_id)
+    live_b, value_b = pick(second_id)
+    masked_a = jnp.where(live_a, value_a, NEGATIVE)
+    masked_b = jnp.where(live_b, value_b, NEGATIVE)
+    peak = jnp.max(jnp.maximum(masked_a, masked_b), axis=1, keepdims=True)
+    total = jnp.sum(
+        jnp.where(live_a, jnp.exp(masked_a - peak), 0.0)
+        + jnp.where(live_b, jnp.exp(masked_b - peak), 0.0),
+        axis=1,
+        keepdims=True,
+    )
+    half = lax.broadcasted_iota(jnp.int32, (group, LANES), 1) < LANES // 2
+    part_send[...] = jnp.where(half, peak, total)
+    share_part = pltpu.make_async_remote_copy(
+        src_ref=part_send,
+        dst_ref=part_recv,
+        send_sem=pair_send_sem.at[1],
+        recv_sem=pair_recv_sem.at[1],
+        device_id={"cls": 1 - side},
+        device_id_type=MESH,
+    )
+    share_part.start()
+    share_part.wait()
+    theirs = part_recv[...]
+    theirs = jnp.concatenate([theirs[part_dev:, :], theirs[:part_dev, :]], axis=0)
+    their_peak = theirs[:, :1]
+    their_total = theirs[:, LANES // 2 : LANES // 2 + 1]
+    top = jnp.maximum(peak, their_peak)
+    both = total * jnp.exp(peak - top) + their_total * jnp.exp(their_peak - top)
+    evidence = top + jnp.log(both)
+    corner = lax.broadcasted_iota(jnp.int32, (group, LANES), 1) == lax.broadcasted_iota(
+        jnp.int32, (group, LANES), 0
+    )
+    evidence_row = jnp.sum(jnp.where(corner, evidence, 0.0), axis=0, keepdims=True)
+    evidence_ref[...] = evidence_row[:, :part_dev]
+
+    posterior = jnp.concatenate(
+        [
+            jnp.where(live_a, jnp.exp(masked_a - evidence), 0.0),
+            jnp.where(live_b, jnp.exp(masked_b - evidence), 0.0),
+        ],
+        axis=0,
+    ).astype(jnp.bfloat16)
+    weight = jnp.sum(posterior.astype(jnp.float32), axis=1, keepdims=True)
+    filters = (weight * jnp.concatenate([quad_group, quad_group], axis=0)).astype(jnp.bfloat16)
+    terms = jnp.dot(posterior, framed[...], preferred_element_type=jnp.float32).astype(
+        jnp.bfloat16
+    )
+    low_lanes = lax.broadcasted_iota(jnp.int32, (pairs, LANES), 1) < cycles
+    for target in range(doms):
+        begin = target * share // LANES * LANES
+        here = slice(target * pairs, (target + 1) * pairs)
+        if target * share == begin:
+            edge = begin + wide - LANES
+            stage[here, : wide - LANES] = terms[:, begin:edge]
+            stage[here, wide - LANES :] = jnp.where(low_lanes, terms[:, edge : edge + LANES], filters)
+        else:
+            stage[here, :LANES] = jnp.where(low_lanes, filters, terms[:, begin : begin + LANES])
+            stage[here, LANES:] = terms[:, begin + LANES : begin + wide]
+    copies = []
+    for step, peer in enumerate(peers):
+        copy = pltpu.make_async_remote_copy(
+            src_ref=stage.at[pl.ds(pl.multiple_of(peer * pairs, pairs), pairs), :],
+            dst_ref=arrived.at[mine, :],
+            send_sem=data_send_sem.at[step],
+            recv_sem=data_recv_sem.at[step],
+            device_id={"dom": peer},
+            device_id_type=MESH,
+        )
+        copy.start()
+        copies.append(copy)
+    arrived[mine, :] = stage[mine, :]
+
+    for copy in id_copies:
+        copy.wait()
+    ids = jnp.broadcast_to(
+        ids_recv[...].astype(jnp.float32)[:, :1], (doms * pairs, class_block)
+    )
+    column = lax.broadcasted_iota(jnp.int32, (doms * pairs, class_block), 1).astype(jnp.float32)
+    chosen = jnp.where(ids == column, 1.0, 0.0).astype(jnp.bfloat16)
+    for copy in copies:
+        copy.wait()
+    contract_first = (((0,), (0,)), ((), ()))
+    late = lax.rem(me, 2) == 1
+    everything = arrived[...]
+    sums = lax.dot_general(
+        everything, chosen, contract_first, preferred_element_type=jnp.float32
+    )
+    sums_ref[...] = jnp.where(late, sums[wide - share :, :], sums[:share, :])
+    filter_part = jnp.where(late, everything[:, :LANES], everything[:, wide - LANES :])
+    filter_sums = lax.dot_general(
+        chosen, filter_part, contract_first, preferred_element_type=jnp.float32
+    )
+    weight_ref[...] = jnp.where(late, filter_sums[:, :cycles], filter_sums[:, cycles:])
+
+
+def paired_shards(images, ctf, inv_noise, classes, candidates):
+    doms = lax.axis_size("dom")
+    part_dev, features = images.shape
+    cycles = ctf.shape[1]
+    class_block = classes.shape[0]
+    shift = features // ROTATIONS
+    group = 2 * part_dev
+    rows = ROTATIONS * group
+    pairs = TOP_CAND * group
+    share = features // doms
+    wide = share + cycles
+    own_rows = ROTATIONS * part_dev + 16
+    f32, bf16 = jnp.float32, jnp.bfloat16
+    vmem = pl.BlockSpec(memory_space=pltpu.VMEM)
+    sums, weight, evidence = pl.pallas_call(
+        functools.partial(estep_kernel, doms),
+        out_shape=(
+            jax.ShapeDtypeStruct((share, class_block), f32),
+            jax.ShapeDtypeStruct((class_block, cycles), f32),
+            jax.ShapeDtypeStruct((1, part_dev), f32),
+        ),
+        in_specs=[vmem] * 4 + [pl.BlockSpec(memory_space=pl.ANY)],
+        out_specs=(vmem, vmem, vmem),
+        scratch_shapes=[
+            pltpu.VMEM((class_block, features), bf16),
+            pltpu.VMEM((own_rows, shift), f32),
+            pltpu.VMEM((own_rows, shift), bf16),
+            pltpu.VMEM((own_rows, shift), bf16),
+            pltpu.VMEM((own_rows, shift), f32),
+            pltpu.VMEM((rows, shift), f32),
+            pltpu.VMEM((2 * rows, shift), bf16),
+            pltpu.VMEM((2 * rows, shift), bf16),
+            pltpu.VMEM((rows, features), bf16),
+            pltpu.VMEM((group, LANES), f32),
+            pltpu.VMEM((group, LANES), f32),
+            pltpu.VMEM((pairs, LANES), bf16),
+            pltpu.VMEM((doms * pairs, LANES), bf16),
+            pltpu.VMEM((doms * pairs, wide), bf16),
+            pltpu.VMEM((doms * pairs, wide), bf16),
+            pltpu.SemaphoreType.DMA,
+            pltpu.SemaphoreType.DMA((2,)),
+            pltpu.SemaphoreType.DMA((2,)),
+            pltpu.SemaphoreType.DMA((doms - 1,)),
+            pltpu.SemaphoreType.DMA((doms - 1,)),
+            pltpu.SemaphoreType.DMA((doms - 1,)),
+            pltpu.SemaphoreType.DMA((doms - 1,)),
+        ],
+        compiler_params=pltpu.CompilerParams(
+            collective_id=0, has_side_effects=True, vmem_limit_bytes=40 * 1024 * 1024
+        ),
+    )(images, ctf, inv_noise[None, :], candidates, classes)
+    return sums, weight, evidence.reshape(part_dev)
+
+
+def pick_plan(images, ctf, inv_noise, classes, candidates):
+    doms = lax.axis_size("dom")
+    part_dev, features = images.shape
+    cycles = ctf.shape[1]
+    fits = (
+        lax.axis_size("cls") == 2
+        and part_dev == 4
+        and 2 * cycles == LANES
+        and features == ROTATIONS * 2 * LANES
+        and doms % 2 == 0
+        and (features // doms) % LANES == cycles
+        and classes.shape[0] <= 256
+    )
+    plan = paired_shards if fits else shards
+    return plan(images, ctf, inv_noise, classes, candidates)
+
+
 def solution(mesh):
     in_specs = (
         P(("dom", "cls"), None),
@@ -153,4 +487,6 @@
         P(("dom", "cls"), None),
     )
     out_specs = (P("dom", "cls"), P("cls", None), P(("dom", "cls")))
-    return jax.shard_map(shards, mesh=mesh, in_specs=in_specs, out_specs=out_specs, check_vma=False)
+    return jax.shard_map(
+        pick_plan, mesh=mesh, in_specs=in_specs, out_specs=out_specs, check_vma=False
+    )

time: 1610 us -> 31.2 us (0.02)
  the two profiles are of different devices: /device:TPU:1 before, /device:TPU:11 now
where the time goes in v1:
time: 31.2 us; the launch traced here: 31 us
  Pallas kernels  23.1 us (74%)
  local copies, waits for them, and re-layouts  7.26 us (23%)
  between operations  0.64 us (2%)
    pallas_call x1, Pallas kernels, paired_shards(): pl.pallas_call(functools.partial(estep_kernel, doms), out_shape=(jax.Shap...  23.1 us
    unnamed x12, local copies, waits for them, and re-layouts  7.26 us

profile of v1, /device:TPU:11, one launch (start us, length us, event | category | flops | bytes accessed | tf_op | source)
XLA Modules:
  0.0 31.0 jit_solution(16485506681436266444)
XLA Ops:
  0.6 0.8 %copy.8.cand_ref = s32[4,2]{1,0:T(4,128)S(1)} copy(s32[4,2]{0,1:T(2,128)} %param.9) | data formatting | bytes 64 | tf_op args[4]
  1.4 0.0 copy-start
  1.4 2.0 %copy-done = bf16[200,9216]{1,0:T(8,128)(2,1)S(1)} copy-done((bf16[200,9216]{1,0:T(8,128)(2,1)S(1)}, bf16[200,9216]{1,0:T(8,128)(2,1)}, u32[]{:S(2)}) %copy-start) | copy-done | bytes 3686424
  3.4 0.0 copy-start.1
  3.4 0.9 %copy-done.1 = bf16[4,9216]{1,0:T(4,128)(2,1)S(1)} copy-done((bf16[4,9216]{1,0:T(4,128)(2,1)S(1)}, bf16[4,9216]{1,0:T(4,128)(2,1)}, u32[]{:S(2)}) %copy-start.1) | copy-done | bytes 73752
  4.3 0.0 copy-start.2
  4.3 0.7 %copy-done.2 = f32[4,64]{1,0:T(4,128)S(1)} copy-done((f32[4,64]{1,0:T(4,128)S(1)}, f32[4,64]{1,0:T(4,128)}, u32[]{:S(2)}) %copy-start.2) | copy-done | bytes 1048
  5.0 0.0 copy-start.3
  5.0 0.7 %copy-done.3 = f32[64]{0:T(128)S(1)} copy-done((f32[64]{0:T(128)S(1)}, f32[64]{0:T(128)}, u32[]{:S(2)}) %copy-start.3) | copy-done | bytes 280
  5.7 23.1 %shard_map.76 = (f32[576,200]{1,0:T(8,128)S(1)}, f32[200,64]{1,0:T(8,128)S(1)}, f32[1,4]{1,0:T(1,128)S(1)}) custom-call(bf16[4,9216]{1,0:T(4,128)(2,1)S(1)} %copy-done.1, f32[4,64]{1,0:T(4,128)S(1)} %copy-done.2, f32[1,64]{1,0:T(1,128)S(1)} %bitcast.2, s32[4,2]{1,0:T(4,128)S(1)} %copy.8.cand_ref, bf16[200,9216]{1,0:T(8,128)(2,1)S(1)} %copy-done), custom_call_target="tpu_custom_call" | custom-call | tf_op jit(solution)/shard_map/pallas_call | solution.py:424
  28.7 1.0 %copy.9 = f32[576,200]{0,1:T(8,128)} copy(f32[576,200]{1,0:T(8,128)S(1)} %get-tuple-element.9) | data formatting | bytes 921600
  29.7 0.7 %copy.10 = f32[200,64]{0,1:T(8,128)} copy(f32[200,64]{1,0:T(8,128)S(1)} %get-tuple-element.10) | data formatting | bytes 102400
  30.5 0.5 %copy.12 = f32[4]{0:T(128)} copy(f32[4]{0:T(128)S(1)} %bitcast.3) | data formatting | bytes 32
Async XLA Ops:
  1.4 2.0 %copy-start = (bf16[200,9216]{1,0:T(8,128)(2,1)S(1)}, bf16[200,9216]{1,0:T(8,128)(2,1)}, u32[]{:S(2)}) copy-start(bf16[200,9216]{1,0:T(8,128)(2,1)} %classes_ref.1) | copy-start | bytes 11059204
  3.4 0.9 %copy-start.1 = (bf16[4,9216]{1,0:T(4,128)(2,1)S(1)}, bf16[4,9216]{1,0:T(4,128)(2,1)}, u32[]{:S(2)}) copy-start(bf16[4,9216]{1,0:T(4,128)(2,1)} %images_ref.1) | copy-start | bytes 221188
  4.3 0.7 %copy-start.2 = (f32[4,64]{1,0:T(4,128)S(1)}, f32[4,64]{1,0:T(4,128)}, u32[]{:S(2)}) copy-start(f32[4,64]{1,0:T(4,128)} %ctf_ref.1) | copy-start | bytes 3076
  5.0 0.7 %copy-start.3 = (f32[64]{0:T(128)S(1)}, f32[64]{0:T(128)}, u32[]{:S(2)}) copy-start(f32[64]{0:T(128)} %param.7) | copy-start | bytes 772

commit v2 on v1

--- a/solution.py
+++ b/solution.py
@@ -158,10 +158,14 @@
     noise_ref,
     cand_ref,
     classes_ref,
-    sums_ref,
-    weight_ref,
+    arrived,
+    chosen_ref,
     evidence_ref,
     held,
+    images_vmem,
+    ctf_vmem,
+    noise_vmem,
+    cand_vmem,
     own_wide,
     own_send,
     other_recv,
@@ -175,7 +179,6 @@
     ids_send,
     ids_recv,
     stage,
-    arrived,
     load_sem,
     pair_send_sem,
     pair_recv_sem,
@@ -198,30 +201,47 @@
     wide = stage.shape[1]
     peers = [lax.rem(me + step, doms) for step in range(1, doms)]
 
-    load = pltpu.make_async_copy(classes_ref, held, load_sem)
-    load.start()
+    loads = [
+        pltpu.make_async_copy(source, target, load_sem.at[place])
+        for place, (source, target) in enumerate(
+            [
+                (cand_ref, cand_vmem),
+                (noise_ref, noise_vmem),
+                (ctf_ref, ctf_vmem),
+                (images_ref, images_vmem),
+                (classes_ref, held),
+            ]
+        )
+    ]
+    for load in loads:
+        load.start()
     barrier = pltpu.get_barrier_semaphore()
     pl.semaphore_signal(barrier, inc=1, device_id={"cls": 1 - side}, device_id_type=MESH)
     for peer in peers:
         pl.semaphore_signal(barrier, inc=1, device_id={"dom": peer}, device_id_type=MESH)
 
-    ctf = ctf_ref[...]
-    noise = noise_ref[...]
+    for load in loads[:4]:
+        load.wait()
+    ctf = ctf_vmem[...]
+    noise = noise_vmem[...]
     factor = jnp.concatenate([ctf * noise] * (shift // cycles), axis=1)
     quad = (ctf * ctf * noise).astype(jnp.bfloat16).astype(jnp.float32)
-    cand = cand_ref[...]
+    cand = cand_vmem[...].astype(jnp.float32)
+    square = (part_dev, part_dev)
+    same = lax.broadcasted_iota(jnp.int32, square, 0) == lax.broadcasted_iota(jnp.int32, square, 1)
 
     def local_ids(block, column):
-        local = cand[:, column : column + 1] - block * class_block
-        inside = (local >= 0) & (local < class_block)
-        local = jnp.where(inside, local, -1).astype(jnp.float32)
-        return jnp.broadcast_to(local, (part_dev, cycles))
+        ids = jnp.broadcast_to(cand[column : column + 1, :], square)
+        ids = jnp.sum(jnp.where(same, ids, 0.0), axis=1, keepdims=True)
+        local = ids - (block * class_block).astype(jnp.float32)
+        inside = (local >= 0.0) & (local < class_block)
+        return jnp.broadcast_to(jnp.where(inside, local, -1.0), (part_dev, cycles))
 
     def extras(block):
         return jnp.concatenate([quad, quad, local_ids(block, 0), local_ids(block, 1)], axis=1)
 
     for turn in range(ROTATIONS):
-        piece = images_ref[:, turn * shift : (turn + 1) * shift].astype(jnp.float32) * factor
+        piece = images_vmem[:, turn * shift : (turn + 1) * shift].astype(jnp.float32) * factor
         piece = piece.astype(jnp.bfloat16).astype(jnp.float32)
         own_wide[turn * part_dev : (turn + 1) * part_dev, :] = piece
         group_wide[turn * group : turn * group + part_dev, :] = piece
@@ -240,7 +260,7 @@
     )
     swap.start()
 
-    load.wait()
+    loads[4].wait()
     energy = jnp.zeros((class_block, LANES), jnp.float32)
     for start in range(0, features, LANES):
         part = held[:, start : start + LANES].astype(jnp.float32)
@@ -359,17 +379,11 @@
     terms = jnp.dot(posterior, framed[...], preferred_element_type=jnp.float32).astype(
         jnp.bfloat16
     )
-    low_lanes = lax.broadcasted_iota(jnp.int32, (pairs, LANES), 1) < cycles
     for target in range(doms):
-        begin = target * share // LANES * LANES
         here = slice(target * pairs, (target + 1) * pairs)
-        if target * share == begin:
-            edge = begin + wide - LANES
-            stage[here, : wide - LANES] = terms[:, begin:edge]
-            stage[here, wide - LANES :] = jnp.where(low_lanes, terms[:, edge : edge + LANES], filters)
-        else:
-            stage[here, :LANES] = jnp.where(low_lanes, filters, terms[:, begin : begin + LANES])
-            stage[here, LANES:] = terms[:, begin + LANES : begin + wide]
+        stage[here, :] = jnp.concatenate(
+            [terms[:, target * share : (target + 1) * share], filters[:, :cycles]], axis=1
+        )
     copies = []
     for step, peer in enumerate(peers):
         copy = pltpu.make_async_remote_copy(
@@ -390,21 +404,27 @@
         ids_recv[...].astype(jnp.float32)[:, :1], (doms * pairs, class_block)
     )
     column = lax.broadcasted_iota(jnp.int32, (doms * pairs, class_block), 1).astype(jnp.float32)
-    chosen = jnp.where(ids == column, 1.0, 0.0).astype(jnp.bfloat16)
+    chosen_ref[...] = jnp.where(ids == column, 1.0, 0.0).astype(jnp.bfloat16)
     for copy in copies:
         copy.wait()
+
+
+def sums_kernel(arrived, chosen, evidence_in, sums_ref, weight_ref, evidence_ref):
+    share = sums_ref.shape[1]
+    cycles = weight_ref.shape[0]
     contract_first = (((0,), (0,)), ((), ()))
-    late = lax.rem(me, 2) == 1
-    everything = arrived[...]
+    evidence_ref[...] = evidence_in[...]
     sums = lax.dot_general(
-        everything, chosen, contract_first, preferred_element_type=jnp.float32
-    )
-    sums_ref[...] = jnp.where(late, sums[wide - share :, :], sums[:share, :])
-    filter_part = jnp.where(late, everything[:, :LANES], everything[:, wide - LANES :])
+        chosen[...], arrived[...], contract_first, preferred_element_type=jnp.float32
+    )
+    sums_ref[...] = sums[:, :share]
     filter_sums = lax.dot_general(
-        chosen, filter_part, contract_first, preferred_element_type=jnp.float32
-    )
-    weight_ref[...] = jnp.where(late, filter_sums[:, :cycles], filter_sums[:, cycles:])
+        arrived[:, share - cycles :],
+        chosen[...],
+        contract_first,
+        preferred_element_type=jnp.float32,
+    )
+    weight_ref[...] = filter_sums[cycles:, :]
 
 
 def paired_shards(images, ctf, inv_noise, classes, candidates):
@@ -421,17 +441,21 @@
     own_rows = ROTATIONS * part_dev + 16
     f32, bf16 = jnp.float32, jnp.bfloat16
     vmem = pl.BlockSpec(memory_space=pltpu.VMEM)
-    sums, weight, evidence = pl.pallas_call(
+    arrived, chosen, evidence = pl.pallas_call(
         functools.partial(estep_kernel, doms),
         out_shape=(
-            jax.ShapeDtypeStruct((share, class_block), f32),
-            jax.ShapeDtypeStruct((class_block, cycles), f32),
+            jax.ShapeDtypeStruct((doms * pairs, wide), bf16),
+            jax.ShapeDtypeStruct((doms * pairs, class_block), bf16),
             jax.ShapeDtypeStruct((1, part_dev), f32),
         ),
-        in_specs=[vmem] * 4 + [pl.BlockSpec(memory_space=pl.ANY)],
+        in_specs=[pl.BlockSpec(memory_space=pltpu.HBM)] * 5,
         out_specs=(vmem, vmem, vmem),
         scratch_shapes=[
             pltpu.VMEM((class_block, features), bf16),
+            pltpu.VMEM((part_dev, features), bf16),
+            pltpu.VMEM((part_dev, cycles), f32),
+            pltpu.VMEM((1, cycles), f32),
+            pltpu.VMEM((TOP_CAND, part_dev), jnp.int32),
             pltpu.VMEM((own_rows, shift), f32),
             pltpu.VMEM((own_rows, shift), bf16),
             pltpu.VMEM((own_rows, shift), bf16),
@@ -445,8 +469,7 @@
             pltpu.VMEM((pairs, LANES), bf16),
             pltpu.VMEM((doms * pairs, LANES), bf16),
             pltpu.VMEM((doms * pairs, wide), bf16),
-            pltpu.VMEM((doms * pairs, wide), bf16),
-            pltpu.SemaphoreType.DMA,
+            pltpu.SemaphoreType.DMA((5,)),
             pltpu.SemaphoreType.DMA((2,)),
             pltpu.SemaphoreType.DMA((2,)),
             pltpu.SemaphoreType.DMA((doms - 1,)),
@@ -455,10 +478,21 @@
             pltpu.SemaphoreType.DMA((doms - 1,)),
         ],
         compiler_params=pltpu.CompilerParams(
-            collective_id=0, has_side_effects=True, vmem_limit_bytes=40 * 1024 * 1024
+            collective_id=0, has_side_effects=True, vmem_limit_bytes=63 * 1024 * 1024
         ),
-    )(images, ctf, inv_noise[None, :], candidates, classes)
-    return sums, weight, evidence.reshape(part_dev)
+    )(images, ctf, inv_noise[None, :], candidates.T, classes)
+    sums, weight, evidence = pl.pallas_call(
+        sums_kernel,
+        out_shape=(
+            jax.ShapeDtypeStruct((class_block, share), f32),
+            jax.ShapeDtypeStruct((cycles, class_block), f32),
+            jax.ShapeDtypeStruct((1, part_dev), f32),
+        ),
+        in_specs=[vmem] * 3,
+        out_specs=(vmem, vmem, vmem),
+        compiler_params=pltpu.CompilerParams(vmem_limit_bytes=63 * 1024 * 1024),
+    )(arrived, chosen, evidence)
+    return sums.T, weight.T, evidence.reshape(part_dev)
 
 
 def pick_plan(images, ctf, inv_noise, classes, candidates):

time: 31.2 us -> 26.2 us (0.84)
  local copies, waits for them, and re-layouts: 7.26 us -> 0 us
  Pallas kernels: 23.1 us -> 25.4 us
    unnamed x12 -> x0, local copies, waits for them, and re-layouts: 7.26 us -> none
    pallas_call x0 -> x1, Pallas kernels: none -> 2.14 us  [paired_shards(): pl.pallas_call(sums_kernel, out_shape=(jax.ShapeDtypeStruct((class_block,...]
where the time goes in v2:
time: 26.2 us; the launch traced here: 26 us
  Pallas kernels  25.4 us (97%)
  between operations  0.64 us (2%)
    pallas_call x1, Pallas kernels, paired_shards(): pl.pallas_call(functools.partial(estep_kernel, doms), out_shape=(jax.Shap...  23.3 us
    pallas_call x1, Pallas kernels, paired_shards(): pl.pallas_call(sums_kernel, out_shape=(jax.ShapeDtypeStruct((class_block,...  2.14 us

profile of v2, /device:TPU:11, one launch (start us, length us, event | category | flops | bytes accessed | tf_op | source)
XLA Modules:
  0.0 26.0 jit_solution(10176327761277517413)
XLA Ops:
  0.6 23.3 %shard_map.76 = (bf16[256,640]{1,0:T(8,128)(2,1)}, bf16[256,200]{1,0:T(8,128)(2,1)}, f32[1,4]{1,0:T(1,128)}) custom-call(bf16[4,9216]{1,0:T(4,128)(2,1)} %images_ref.1, f32[4,64]{1,0:T(4,128)} %ctf_ref.1, f32[1,64]{1,0:T(1,128)} %bitcast.6, s32[2,4]{1,0:T(2,128)} %bitcast.5, bf16[200,9216]{1,0:T(8,128)(2,1)} %classes_ref.1), custom_call_target="tpu_custom_call" | custom-call | tf_op jit(solution)/shard_map/pallas_call | solution.py:444
  23.9 2.1 %shard_map.77 = (f32[200,576]{1,0:T(8,128)}, f32[64,200]{1,0:T(8,128)}, f32[1,4]{1,0:T(1,128)}) custom-call(bf16[256,640]{1,0:T(8,128)(2,1)} %get-tuple-element.9.arrived, bf16[256,200]{1,0:T(8,128)(2,1)} %get-tuple-element.10.chosen, f32[1,4]{1,0:T(1,128)} %get-tuple-element.11.evidence_in), custom_call_target="tpu_custom_call" | custom-call | tf_op jit(solution)/shard_map/pallas_call | solution.py:484

commit v3 on v2

--- a/solution.py
+++ b/solution.py
@@ -169,11 +169,9 @@
     own_wide,
     own_send,
     other_recv,
-    other_wide,
-    group_wide,
-    twin_even,
-    twin_odd,
-    framed,
+    twins,
+    own_framed,
+    other_framed,
     part_send,
     part_recv,
     ids_send,
@@ -192,11 +190,10 @@
     part_dev, features = images_ref.shape
     cycles = ctf_ref.shape[1]
     class_block = held.shape[0]
-    shift = framed.shape[1] // ROTATIONS
+    shift = features // ROTATIONS
     group = 2 * part_dev
-    rows = ROTATIONS * group
     pairs = TOP_CAND * group
-    own_rows = ROTATIONS * part_dev
+    rows = ROTATIONS * part_dev
     share = features // doms
     wide = stage.shape[1]
     peers = [lax.rem(me + step, doms) for step in range(1, doms)]
@@ -244,9 +241,8 @@
         piece = images_vmem[:, turn * shift : (turn + 1) * shift].astype(jnp.float32) * factor
         piece = piece.astype(jnp.bfloat16).astype(jnp.float32)
         own_wide[turn * part_dev : (turn + 1) * part_dev, :] = piece
-        group_wide[turn * group : turn * group + part_dev, :] = piece
-    own_wide[own_rows : own_rows + 16, :] = jnp.zeros((16, shift), jnp.float32)
-    own_wide[own_rows : own_rows + part_dev, :] = extras(1 - side)
+    own_wide[rows : rows + 16, :] = jnp.zeros((16, shift), jnp.float32)
+    own_wide[rows : rows + part_dev, :] = extras(1 - side)
     own_send[...] = own_wide[...].astype(jnp.bfloat16)
 
     pl.semaphore_wait(barrier, doms)
@@ -266,19 +262,61 @@
         part = held[:, start : start + LANES].astype(jnp.float32)
         energy = energy + part * part
 
+    def frame(values, framed):
+        doubled = jnp.concatenate([values, values], axis=0)
+        for late in range(4):
+            cut = late * part_dev
+            moved = jnp.concatenate([doubled[cut:], doubled[:cut]], axis=0) if cut else doubled
+            twins[late] = moved.astype(jnp.bfloat16)
+        for turn in range(ROTATIONS):
+            begin = turn // 4 * 4 * part_dev
+            framed[:, turn * shift : (turn + 1) * shift] = twins[turn % 4, begin : begin + rows, :]
+
+    contract_last = (((1,), (1,)), ((), ()))
+    lane = lax.broadcasted_iota(jnp.int32, (part_dev, rows), 1)
+    own_lane = (lane & (part_dev - 1)) == lax.broadcasted_iota(jnp.int32, (part_dev, rows), 0)
+    class_row = lax.broadcasted_iota(jnp.int32, (class_block, rows), 0).astype(jnp.float32)
+
+    def score(framed, info):
+        cross = lax.dot_general(
+            held[...], framed[...], contract_last, preferred_element_type=jnp.float32
+        )
+        norm = lax.dot_general(
+            energy,
+            jnp.concatenate([info[:, :LANES]] * ROTATIONS, axis=0),
+            contract_last,
+            precision=lax.Precision.HIGHEST,
+            preferred_element_type=jnp.float32,
+        )
+        logits = cross - 0.5 * norm
+        found = []
+        for place in range(TOP_CAND):
+            ids = info[:, (2 + place) * cycles : (2 + place) * cycles + 1]
+            wanted = jnp.sum(jnp.where(own_lane, ids, 0.0), axis=0, keepdims=True)
+            value = jnp.sum(jnp.where(class_row == wanted, logits, 0.0), axis=0, keepdims=True)
+            live = own_lane & (ids >= 0.0)
+            found.append((live, jnp.where(live, value, NEGATIVE)))
+        peak = functools.reduce(jnp.maximum, [value for live, value in found])
+        peak = jnp.max(peak, axis=1, keepdims=True)
+        total = sum(jnp.where(live, jnp.exp(value - peak), 0.0) for live, value in found)
+        return found, peak, jnp.sum(total, axis=1, keepdims=True)
+
+    own_info = extras(side)
+    frame(own_wide[:rows, :], own_framed)
+    own_found, own_peak, own_total = score(own_framed, own_info)
+
     swap.wait()
-    other_wide[...] = other_recv[...].astype(jnp.float32)
-    for turn in range(ROTATIONS):
-        group_wide[turn * group + part_dev : (turn + 1) * group, :] = other_wide[
-            turn * part_dev : (turn + 1) * part_dev, :
-        ]
-    info = jnp.concatenate([extras(side), other_wide[own_rows : own_rows + part_dev, :]], axis=0)
-    quad_group = info[:, :LANES]
-    first_id = info[:, 2 * cycles : 2 * cycles + 1]
-    second_id = info[:, 3 * cycles : 3 * cycles + 1]
-
-    ids_send[...] = jnp.broadcast_to(
-        jnp.concatenate([first_id, second_id], axis=0), (pairs, LANES)
+    other_all = other_recv[...].astype(jnp.float32)
+    other_info = other_all[rows : rows + part_dev, :]
+    by_pair = [own_info, own_info, other_info, other_info]
+    ids_send[...] = jnp.concatenate(
+        [
+            jnp.broadcast_to(
+                info[:, (2 + place % 2) * cycles : (2 + place % 2) * cycles + 1], (part_dev, LANES)
+            )
+            for place, info in enumerate(by_pair)
+        ],
+        axis=0,
     ).astype(jnp.bfloat16)
     mine = pl.ds(pl.multiple_of(me * pairs, pairs), pairs)
     ids_recv[mine, :] = ids_send[...]
@@ -295,53 +333,10 @@
         copy.start()
         id_copies.append(copy)
 
-    even = group_wide[...].astype(jnp.bfloat16)
-    odd = jnp.concatenate([group_wide[group:, :], group_wide[:group, :]], axis=0).astype(
-        jnp.bfloat16
-    )
-    twin_even[:rows, :] = even
-    twin_even[rows:, :] = even
-    twin_odd[:rows, :] = odd
-    twin_odd[rows:, :] = odd
-    for turn in range(ROTATIONS):
-        window = twin_odd if turn % 2 else twin_even
-        begin = (turn - turn % 2) * group
-        framed[:, turn * shift : (turn + 1) * shift] = window[begin : begin + rows, :]
-
-    contract_last = (((1,), (1,)), ((), ()))
-    cross = lax.dot_general(
-        held[...], framed[...], contract_last, preferred_element_type=jnp.float32
-    )
-    norm = lax.dot_general(
-        energy,
-        jnp.concatenate([quad_group] * ROTATIONS, axis=0),
-        contract_last,
-        precision=lax.Precision.HIGHEST,
-        preferred_element_type=jnp.float32,
-    )
-    logits = cross - 0.5 * norm
-
-    lane = lax.broadcasted_iota(jnp.int32, (group, rows), 1)
-    own_lane = (lane & (group - 1)) == lax.broadcasted_iota(jnp.int32, (group, rows), 0)
-    class_row = lax.broadcasted_iota(jnp.int32, (class_block, rows), 0).astype(jnp.float32)
-
-    def pick(ids):
-        wanted = jnp.sum(jnp.where(own_lane, ids, 0.0), axis=0, keepdims=True)
-        value = jnp.sum(jnp.where(class_row == wanted, logits, 0.0), axis=0, keepdims=True)
-        live = own_lane & (ids >= 0.0)
-        return live, jnp.broadcast_to(value, (group, rows))
-
-    live_a, value_a = pick(first_id)
-    live_b, value_b = pick(second_id)
-    masked_a = jnp.where(live_a, value_a, NEGATIVE)
-    masked_b = jnp.where(live_b, value_b, NEGATIVE)
-    peak = jnp.max(jnp.maximum(masked_a, masked_b), axis=1, keepdims=True)
-    total = jnp.sum(
-        jnp.where(live_a, jnp.exp(masked_a - peak), 0.0)
-        + jnp.where(live_b, jnp.exp(masked_b - peak), 0.0),
-        axis=1,
-        keepdims=True,
-    )
+    frame(other_all[:rows, :], other_framed)
+    other_found, other_peak, other_total = score(other_framed, other_info)
+    peak = jnp.concatenate([own_peak, other_peak], axis=0)
+    total = jnp.concatenate([own_total, other_total], axis=0)
     half = lax.broadcasted_iota(jnp.int32, (group, LANES), 1) < LANES // 2
     part_send[...] = jnp.where(half, peak, total)
     share_part = pltpu.make_async_remote_copy(
@@ -367,35 +362,51 @@
     evidence_row = jnp.sum(jnp.where(corner, evidence, 0.0), axis=0, keepdims=True)
     evidence_ref[...] = evidence_row[:, :part_dev]
 
-    posterior = jnp.concatenate(
+    def posteriors(found, evidence):
+        parts = [jnp.where(live, jnp.exp(value - evidence), 0.0) for live, value in found]
+        return jnp.concatenate(parts, axis=0).astype(jnp.bfloat16)
+
+    own_post = posteriors(own_found, evidence[:part_dev])
+    other_post = posteriors(other_found, evidence[part_dev:])
+    weight = jnp.concatenate(
         [
-            jnp.where(live_a, jnp.exp(masked_a - evidence), 0.0),
-            jnp.where(live_b, jnp.exp(masked_b - evidence), 0.0),
+            jnp.sum(post.astype(jnp.float32), axis=1, keepdims=True)
+            for post in (own_post, other_post)
         ],
         axis=0,
-    ).astype(jnp.bfloat16)
-    weight = jnp.sum(posterior.astype(jnp.float32), axis=1, keepdims=True)
-    filters = (weight * jnp.concatenate([quad_group, quad_group], axis=0)).astype(jnp.bfloat16)
-    terms = jnp.dot(posterior, framed[...], preferred_element_type=jnp.float32).astype(
-        jnp.bfloat16
-    )
-    for target in range(doms):
-        here = slice(target * pairs, (target + 1) * pairs)
-        stage[here, :] = jnp.concatenate(
-            [terms[:, target * share : (target + 1) * share], filters[:, :cycles]], axis=1
-        )
+    )
+    filters = weight * jnp.concatenate([info[:, :cycles] for info in by_pair], axis=0)
+
+    chips = doms // 2
+    chip, core = me // 2, lax.rem(me, 2)
     copies = []
-    for step, peer in enumerate(peers):
-        copy = pltpu.make_async_remote_copy(
-            src_ref=stage.at[pl.ds(pl.multiple_of(peer * pairs, pairs), pairs), :],
-            dst_ref=arrived.at[mine, :],
-            send_sem=data_send_sem.at[step],
-            recv_sem=data_recv_sem.at[step],
-            device_id={"dom": peer},
-            device_id_type=MESH,
-        )
-        copy.start()
-        copies.append(copy)
+    for step in sorted(range(chips), key=lambda step: -min(step, chips - step)):
+        target = lax.rem(chip + step, chips)
+        lanes = pl.ds(pl.multiple_of(target * 2 * share, LANES), 2 * share)
+        terms = jnp.concatenate(
+            [
+                jnp.dot(own_post, own_framed[:, lanes], preferred_element_type=jnp.float32),
+                jnp.dot(other_post, other_framed[:, lanes], preferred_element_type=jnp.float32),
+            ],
+            axis=0,
+        )
+        for to in range(2):
+            here = pl.ds(pl.multiple_of((2 * target + to) * pairs, pairs), pairs)
+            stage[here, :] = jnp.concatenate(
+                [terms[:, to * share : (to + 1) * share], filters], axis=1
+            ).astype(jnp.bfloat16)
+        for to in range(2 if step else 1):
+            peer = 2 * target + to if step else me + 1 - 2 * core
+            copy = pltpu.make_async_remote_copy(
+                src_ref=stage.at[pl.ds(pl.multiple_of(peer * pairs, pairs), pairs), :],
+                dst_ref=arrived.at[mine, :],
+                send_sem=data_send_sem.at[2 * step + to],
+                recv_sem=data_recv_sem.at[2 * step + core if step else 0],
+                device_id={"dom": peer},
+                device_id_type=MESH,
+            )
+            copy.start()
+            copies.append((copy, 2 * step + to, peer))
     arrived[mine, :] = stage[mine, :]
 
     for copy in id_copies:
@@ -405,8 +416,16 @@
     )
     column = lax.broadcasted_iota(jnp.int32, (doms * pairs, class_block), 1).astype(jnp.float32)
     chosen_ref[...] = jnp.where(ids == column, 1.0, 0.0).astype(jnp.bfloat16)
-    for copy in copies:
-        copy.wait()
+    for copy, place, peer in copies:
+        copy.wait_send()
+        pltpu.make_async_remote_copy(
+            src_ref=stage.at[mine, :],
+            dst_ref=arrived.at[mine, :],
+            send_sem=data_send_sem.at[place],
+            recv_sem=data_recv_sem.at[place],
+            device_id={"dom": peer},
+            device_id_type=MESH,
+        ).wait_recv()
 
 
 def sums_kernel(arrived, chosen, evidence_in, sums_ref, weight_ref, evidence_ref):
@@ -434,11 +453,11 @@
     class_block = classes.shape[0]
     shift = features // ROTATIONS
     group = 2 * part_dev
-    rows = ROTATIONS * group
+    rows = ROTATIONS * part_dev
     pairs = TOP_CAND * group
     share = features // doms
     wide = share + cycles
-    own_rows = ROTATIONS * part_dev + 16
+    own_rows = rows + 16
     f32, bf16 = jnp.float32, jnp.bfloat16
     vmem = pl.BlockSpec(memory_space=pltpu.VMEM)
     arrived, chosen, evidence = pl.pallas_call(
@@ -459,10 +478,8 @@
             pltpu.VMEM((own_rows, shift), f32),
             pltpu.VMEM((own_rows, shift), bf16),
             pltpu.VMEM((own_rows, shift), bf16),
-            pltpu.VMEM((own_rows, shift), f32),
-            pltpu.VMEM((rows, shift), f32),
-            pltpu.VMEM((2 * rows, shift), bf16),
-            pltpu.VMEM((2 * rows, shift), bf16),
+            pltpu.VMEM((4, 2 * rows, shift), bf16),
+            pltpu.VMEM((rows, features), bf16),
             pltpu.VMEM((rows, features), bf16),
             pltpu.VMEM((group, LANES), f32),
             pltpu.VMEM((group, LANES), f32),
@@ -474,8 +491,8 @@
             pltpu.SemaphoreType.DMA((2,)),
             pltpu.SemaphoreType.DMA((doms - 1,)),
             pltpu.SemaphoreType.DMA((doms - 1,)),
-            pltpu.SemaphoreType.DMA((doms - 1,)),
-            pltpu.SemaphoreType.DMA((doms - 1,)),
+            pltpu.SemaphoreType.DMA((doms,)),
+            pltpu.SemaphoreType.DMA((doms,)),
         ],
         compiler_params=pltpu.CompilerParams(
             collective_id=0, has_side_effects=True, vmem_limit_bytes=63 * 1024 * 1024

time: 26.2 us -> 26.9 us (1.027)
  the two profiles are of different devices: /device:TPU:11 before, /device:TPU:1 now
where the time goes in v3:
time: 26.9 us; the launch traced here: 26.4 us
  Pallas kernels  25.8 us (96%)
  between operations  0.64 us (2%)
    pallas_call x1, Pallas kernels, paired_shards(): pl.pallas_call(functools.partial(estep_kernel, doms), out_shape=(jax.Shap...  23.7 us
    pallas_call x1, Pallas kernels, paired_shards(): pl.pallas_call(sums_kernel, out_shape=(jax.ShapeDtypeStruct((class_block,...  2.14 us

profile of v3, /device:TPU:1, one launch (start us, length us, event | category | flops | bytes accessed | tf_op | source)
XLA Modules:
  0.0 26.4 jit_solution(15015959676515909211)
XLA Ops:
  0.6 23.7 %shard_map.76 = (bf16[256,640]{1,0:T(8,128)(2,1)}, bf16[256,200]{1,0:T(8,128)(2,1)}, f32[1,4]{1,0:T(1,128)}) custom-call(bf16[4,9216]{1,0:T(4,128)(2,1)} %images_ref.1, f32[4,64]{1,0:T(4,128)} %ctf_ref.1, f32[1,64]{1,0:T(1,128)} %bitcast.6, s32[2,4]{1,0:T(2,128)} %bitcast.5, bf16[200,9216]{1,0:T(8,128)(2,1)} %classes_ref.1), custom_call_target="tpu_custom_call" | custom-call | tf_op jit(solution)/shard_map/pallas_call | solution.py:463
  24.3 2.1 %shard_map.77 = (f32[200,576]{1,0:T(8,128)}, f32[64,200]{1,0:T(8,128)}, f32[1,4]{1,0:T(1,128)}) custom-call(bf16[256,640]{1,0:T(8,128)(2,1)} %get-tuple-element.9.arrived, bf16[256,200]{1,0:T(8,128)(2,1)} %get-tuple-element.10.chosen, f32[1,4]{1,0:T(1,128)} %get-tuple-element.11.evidence_in), custom_call_target="tpu_custom_call" | custom-call | tf_op jit(solution)/shard_map/pallas_call | solution.py:501

commit v4 on v3

--- a/solution.py
+++ b/solution.py
@@ -184,6 +184,8 @@
     ids_recv_sem,
     data_send_sem,
     data_recv_sem,
+    next_send_sem,
+    next_recv_sem,
 ):
     me = lax.axis_index("dom")
     side = lax.axis_index("cls")
@@ -195,7 +197,6 @@
     pairs = TOP_CAND * group
     rows = ROTATIONS * part_dev
     share = features // doms
-    wide = stage.shape[1]
     peers = [lax.rem(me + step, doms) for step in range(1, doms)]
 
     loads = [
@@ -289,21 +290,18 @@
             preferred_element_type=jnp.float32,
         )
         logits = cross - 0.5 * norm
-        found = []
+        values = []
         for place in range(TOP_CAND):
             ids = info[:, (2 + place) * cycles : (2 + place) * cycles + 1]
             wanted = jnp.sum(jnp.where(own_lane, ids, 0.0), axis=0, keepdims=True)
-            value = jnp.sum(jnp.where(class_row == wanted, logits, 0.0), axis=0, keepdims=True)
-            live = own_lane & (ids >= 0.0)
-            found.append((live, jnp.where(live, value, NEGATIVE)))
-        peak = functools.reduce(jnp.maximum, [value for live, value in found])
-        peak = jnp.max(peak, axis=1, keepdims=True)
-        total = sum(jnp.where(live, jnp.exp(value - peak), 0.0) for live, value in found)
-        return found, peak, jnp.sum(total, axis=1, keepdims=True)
+            values.append(
+                jnp.sum(jnp.where(class_row == wanted, logits, 0.0), axis=0, keepdims=True)
+            )
+        return values
 
     own_info = extras(side)
     frame(own_wide[:rows, :], own_framed)
-    own_found, own_peak, own_total = score(own_framed, own_info)
+    own_values = score(own_framed, own_info)
 
     swap.wait()
     other_all = other_recv[...].astype(jnp.float32)
@@ -334,11 +332,9 @@
         id_copies.append(copy)
 
     frame(other_all[:rows, :], other_framed)
-    other_found, other_peak, other_total = score(other_framed, other_info)
-    peak = jnp.concatenate([own_peak, other_peak], axis=0)
-    total = jnp.concatenate([own_total, other_total], axis=0)
-    half = lax.broadcasted_iota(jnp.int32, (group, LANES), 1) < LANES // 2
-    part_send[...] = jnp.where(half, peak, total)
+    other_values = score(other_framed, other_info)
+    upper = lax.broadcasted_iota(jnp.int32, part_send.shape, 0) == 0
+    part_send[...] = jnp.where(upper, other_values[0], other_values[1])
     share_part = pltpu.make_async_remote_copy(
         src_ref=part_send,
         dst_ref=part_recv,
@@ -350,82 +346,101 @@
     share_part.start()
     share_part.wait()
     theirs = part_recv[...]
-    theirs = jnp.concatenate([theirs[part_dev:, :], theirs[:part_dev, :]], axis=0)
-    their_peak = theirs[:, :1]
-    their_total = theirs[:, LANES // 2 : LANES // 2 + 1]
-    top = jnp.maximum(peak, their_peak)
-    both = total * jnp.exp(peak - top) + their_total * jnp.exp(their_peak - top)
-    evidence = top + jnp.log(both)
-    corner = lax.broadcasted_iota(jnp.int32, (group, LANES), 1) == lax.broadcasted_iota(
-        jnp.int32, (group, LANES), 0
+    first = jnp.where(own_lane, own_values[0] + theirs[0:1, :], NEGATIVE)
+    second = jnp.where(own_lane, own_values[1] + theirs[1:2, :], NEGATIVE)
+    peak = jnp.max(jnp.maximum(first, second), axis=1, keepdims=True)
+    total = jnp.where(own_lane, jnp.exp(first - peak) + jnp.exp(second - peak), 0.0)
+    evidence = peak + jnp.log(jnp.sum(total, axis=1, keepdims=True))
+    corner = lax.broadcasted_iota(jnp.int32, (part_dev, LANES), 1) == lax.broadcasted_iota(
+        jnp.int32, (part_dev, LANES), 0
     )
     evidence_row = jnp.sum(jnp.where(corner, evidence, 0.0), axis=0, keepdims=True)
     evidence_ref[...] = evidence_row[:, :part_dev]
 
-    def posteriors(found, evidence):
-        parts = [jnp.where(live, jnp.exp(value - evidence), 0.0) for live, value in found]
-        return jnp.concatenate(parts, axis=0).astype(jnp.bfloat16)
-
-    own_post = posteriors(own_found, evidence[:part_dev])
-    other_post = posteriors(other_found, evidence[part_dev:])
-    weight = jnp.concatenate(
-        [
-            jnp.sum(post.astype(jnp.float32), axis=1, keepdims=True)
-            for post in (own_post, other_post)
-        ],
-        axis=0,
-    )
-    filters = weight * jnp.concatenate([info[:, :cycles] for info in by_pair], axis=0)
+    posterior = jnp.concatenate(
+        [jnp.where(own_lane, jnp.exp(value - evidence), 0.0) for value in (first, second)], axis=0
+    ).astype(jnp.bfloat16)
+    weight = jnp.sum(posterior.astype(jnp.float32), axis=1, keepdims=True)
+    filters = weight * jnp.concatenate([quad, quad], axis=0)
 
     chips = doms // 2
     chip, core = me // 2, lax.rem(me, 2)
+
+    def across(step):
+        place, bit = 0, 1
+        while bit < chips:
+            digit = lax.rem(chip // bit, 2)
+            place = place + bit * (1 - digit if step & bit else digit)
+            bit *= 2
+        return place
+
+    def to_dom(peer, place, landing):
+        return pltpu.make_async_remote_copy(
+            src_ref=stage.at[peer],
+            dst_ref=arrived.at[me],
+            send_sem=data_send_sem.at[place],
+            recv_sem=data_recv_sem.at[landing],
+            device_id={"dom": peer},
+            device_id_type=MESH,
+        )
+
+    def to_side(source, place, target):
+        return pltpu.make_async_remote_copy(
+            src_ref=source,
+            dst_ref=arrived.at[doms + target],
+            send_sem=next_send_sem.at[place],
+            recv_sem=next_recv_sem.at[place],
+            device_id={"cls": 1 - side},
+            device_id_type=MESH,
+        )
+
+    half = chips // 2
+    order = [step for near in range(1, half) for step in (half + near - 1, near)]
+    order += [chips - 1, 0]
     copies = []
-    for step in sorted(range(chips), key=lambda step: -min(step, chips - step)):
-        target = lax.rem(chip + step, chips)
+    for step in order:
+        target = across(step)
         lanes = pl.ds(pl.multiple_of(target * 2 * share, LANES), 2 * share)
-        terms = jnp.concatenate(
-            [
-                jnp.dot(own_post, own_framed[:, lanes], preferred_element_type=jnp.float32),
-                jnp.dot(other_post, other_framed[:, lanes], preferred_element_type=jnp.float32),
-            ],
-            axis=0,
-        )
+        terms = jnp.dot(posterior, own_framed[:, lanes], preferred_element_type=jnp.float32)
         for to in range(2):
-            here = pl.ds(pl.multiple_of((2 * target + to) * pairs, pairs), pairs)
-            stage[here, :] = jnp.concatenate(
+            stage[2 * target + to] = jnp.concatenate(
                 [terms[:, to * share : (to + 1) * share], filters], axis=1
             ).astype(jnp.bfloat16)
         for to in range(2 if step else 1):
             peer = 2 * target + to if step else me + 1 - 2 * core
-            copy = pltpu.make_async_remote_copy(
-                src_ref=stage.at[pl.ds(pl.multiple_of(peer * pairs, pairs), pairs), :],
-                dst_ref=arrived.at[mine, :],
-                send_sem=data_send_sem.at[2 * step + to],
-                recv_sem=data_recv_sem.at[2 * step + core if step else 0],
-                device_id={"dom": peer},
-                device_id_type=MESH,
-            )
+            landing = 2 * step + core if step else 0
+            copy = to_dom(peer, 2 * step + to, landing)
             copy.start()
-            copies.append((copy, 2 * step + to, peer))
-    arrived[mine, :] = stage[mine, :]
+            copies.append((copy, peer, 2 * step + to))
+    mine_next = to_side(stage.at[me], doms - 1, me)
+    mine_next.start()
+    arrived[me] = stage[me]
+
+    nexts = [mine_next]
+    for place, (copy, peer, landing) in enumerate(copies):
+        to_dom(peer, landing, landing).wait_recv()
+        onward = to_side(arrived.at[peer], place, peer)
+        onward.start()
+        nexts.append(onward)
 
     for copy in id_copies:
         copy.wait()
-    ids = jnp.broadcast_to(
-        ids_recv[...].astype(jnp.float32)[:, :1], (doms * pairs, class_block)
-    )
-    column = lax.broadcasted_iota(jnp.int32, (doms * pairs, class_block), 1).astype(jnp.float32)
-    chosen_ref[...] = jnp.where(ids == column, 1.0, 0.0).astype(jnp.bfloat16)
-    for copy, place, peer in copies:
+    ids = ids_recv[...].astype(jnp.float32)
+    count = doms * pairs // 2
+    for place in range(2):
+        part = [
+            ids[dom * pairs + place * group : dom * pairs + (place + 1) * group, :1]
+            for dom in range(doms)
+        ]
+        part = jnp.broadcast_to(jnp.concatenate(part, axis=0), (count, class_block))
+        column = lax.broadcasted_iota(jnp.int32, (count, class_block), 1).astype(jnp.float32)
+        chosen_ref[place * count : (place + 1) * count, :] = jnp.where(
+            part == column, 1.0, 0.0
+        ).astype(jnp.bfloat16)
+    for copy, peer, landing in copies:
         copy.wait_send()
-        pltpu.make_async_remote_copy(
-            src_ref=stage.at[mine, :],
-            dst_ref=arrived.at[mine, :],
-            send_sem=data_send_sem.at[place],
-            recv_sem=data_recv_sem.at[place],
-            device_id={"dom": peer},
-            device_id_type=MESH,
-        ).wait_recv()
+    for onward in nexts:
+        onward.wait()
 
 
 def sums_kernel(arrived, chosen, evidence_in, sums_ref, weight_ref, evidence_ref):
@@ -463,7 +478,7 @@
     arrived, chosen, evidence = pl.pallas_call(
         functools.partial(estep_kernel, doms),
         out_shape=(
-            jax.ShapeDtypeStruct((doms * pairs, wide), bf16),
+            jax.ShapeDtypeStruct((2 * doms, group, wide), bf16),
             jax.ShapeDtypeStruct((doms * pairs, class_block), bf16),
             jax.ShapeDtypeStruct((1, part_dev), f32),
         ),
@@ -481,16 +496,18 @@
             pltpu.VMEM((4, 2 * rows, shift), bf16),
             pltpu.VMEM((rows, features), bf16),
             pltpu.VMEM((rows, features), bf16),
-            pltpu.VMEM((group, LANES), f32),
-            pltpu.VMEM((group, LANES), f32),
+            pltpu.VMEM((group, rows), f32),
+            pltpu.VMEM((group, rows), f32),
             pltpu.VMEM((pairs, LANES), bf16),
             pltpu.VMEM((doms * pairs, LANES), bf16),
-            pltpu.VMEM((doms * pairs, wide), bf16),
+            pltpu.VMEM((doms, group, wide), bf16),
             pltpu.SemaphoreType.DMA((5,)),
             pltpu.SemaphoreType.DMA((2,)),
             pltpu.SemaphoreType.DMA((2,)),
             pltpu.SemaphoreType.DMA((doms - 1,)),
             pltpu.SemaphoreType.DMA((doms - 1,)),
+            pltpu.SemaphoreType.DMA((doms,)),
+            pltpu.SemaphoreType.DMA((doms,)),
             pltpu.SemaphoreType.DMA((doms,)),
             pltpu.SemaphoreType.DMA((doms,)),
         ],
@@ -508,7 +525,7 @@
         in_specs=[vmem] * 3,
         out_specs=(vmem, vmem, vmem),
         compiler_params=pltpu.CompilerParams(vmem_limit_bytes=63 * 1024 * 1024),
-    )(arrived, chosen, evidence)
+    )(arrived.reshape(doms * pairs, wide), chosen, evidence)
     return sums.T, weight.T, evidence.reshape(part_dev)
 
 
@@ -521,7 +538,8 @@
         and part_dev == 4
         and 2 * cycles == LANES
         and features == ROTATIONS * 2 * LANES
-        and doms % 2 == 0
+        and doms >= 8
+        and doms & (doms - 1) == 0
         and (features // doms) % LANES == cycles
         and classes.shape[0] <= 256
     )

time: 26.9 us -> 28.3 us (1.052)
  the two profiles are of different devices: /device:TPU:1 before, /device:TPU:0 now
where the time goes in v4:
time: 28.3 us; the launch traced here: 28.1 us
  Pallas kernels  27.5 us (97%)
  between operations  0.64 us (2%)
    pallas_call x1, Pallas kernels, paired_shards(): pl.pallas_call(functools.partial(estep_kernel, doms), out_shape=(jax.Shap...  25.3 us
    pallas_call x1, Pallas kernels, paired_shards(): pl.pallas_call(sums_kernel, out_shape=(jax.ShapeDtypeStruct((class_block,...  2.14 us

profile of v4, /device:TPU:0, one launch (start us, length us, event | category | flops | bytes accessed | tf_op | source)
XLA Modules:
  0.0 28.1 jit_solution(8114028708780213933)
XLA Ops:
  0.6 25.3 %shard_map.76 = (bf16[32,8,640]{2,1,0:T(8,128)(2,1)}, bf16[256,200]{1,0:T(8,128)(2,1)}, f32[1,4]{1,0:T(1,128)}) custom-call(bf16[4,9216]{1,0:T(4,128)(2,1)} %images_ref.1, f32[4,64]{1,0:T(4,128)} %ctf_ref.1, f32[1,64]{1,0:T(1,128)} %bitcast.8, s32[2,4]{1,0:T(2,128)} %bitcast.7, bf16[200,9216]{1,0:T(8,128)(2,1)} %classes_ref.1), custom_call_target="tpu_custom_call" | custom-call | tf_op jit(solution)/shard_map/pallas_call | solution.py:478
  26.0 2.1 %shard_map.77 = (f32[200,576]{1,0:T(8,128)}, f32[64,200]{1,0:T(8,128)}, f32[1,4]{1,0:T(1,128)}) custom-call(bf16[256,640]{1,0:T(8,128)(2,1)} %bitcast.6, bf16[256,200]{1,0:T(8,128)(2,1)} %get-tuple-element.10.chosen, f32[1,4]{1,0:T(1,128)} %get-tuple-element.11.evidence_in), custom_call_target="tpu_custom_call" | custom-call | tf_op jit(solution)/shard_map/pallas_call | solution.py:518

commit v5 on v3

--- a/solution.py
+++ b/solution.py
@@ -177,6 +177,7 @@
     ids_send,
     ids_recv,
     stage,
+    pair_sums,
     load_sem,
     pair_send_sem,
     pair_recv_sem,
@@ -308,6 +309,21 @@
     swap.wait()
     other_all = other_recv[...].astype(jnp.float32)
     other_info = other_all[rows : rows + part_dev, :]
+    frame(other_all[:rows, :], other_framed)
+    other_found, other_peak, other_total = score(other_framed, other_info)
+    peak = jnp.concatenate([own_peak, other_peak], axis=0)
+    total = jnp.concatenate([own_total, other_total], axis=0)
+    half = lax.broadcasted_iota(jnp.int32, (group, LANES), 1) < LANES // 2
+    part_send[...] = jnp.where(half, peak, total)
+    share_part = pltpu.make_async_remote_copy(
+        src_ref=part_send,
+        dst_ref=part_recv,
+        send_sem=pair_send_sem.at[1],
+        recv_sem=pair_recv_sem.at[1],
+        device_id={"cls": 1 - side},
+        device_id_type=MESH,
+    )
+    share_part.start()
     by_pair = [own_info, own_info, other_info, other_info]
     ids_send[...] = jnp.concatenate(
         [
@@ -333,21 +349,23 @@
         copy.start()
         id_copies.append(copy)
 
-    frame(other_all[:rows, :], other_framed)
-    other_found, other_peak, other_total = score(other_framed, other_info)
-    peak = jnp.concatenate([own_peak, other_peak], axis=0)
-    total = jnp.concatenate([own_total, other_total], axis=0)
-    half = lax.broadcasted_iota(jnp.int32, (group, LANES), 1) < LANES // 2
-    part_send[...] = jnp.where(half, peak, total)
-    share_part = pltpu.make_async_remote_copy(
-        src_ref=part_send,
-        dst_ref=part_recv,
-        send_sem=pair_send_sem.at[1],
-        recv_sem=pair_recv_sem.at[1],
-        device_id={"cls": 1 - side},
-        device_id_type=MESH,
-    )
-    share_part.start()
+    def raw_weights(found, peak):
+        parts = [jnp.where(live, jnp.exp(value - peak), 0.0) for live, value in found]
+        return jnp.concatenate(parts, axis=0).astype(jnp.bfloat16)
+
+    own_raw = raw_weights(own_found, own_peak)
+    other_raw = raw_weights(other_found, other_peak)
+    raw_weight = jnp.concatenate(
+        [jnp.sum(raw.astype(jnp.float32), axis=1, keepdims=True) for raw in (own_raw, other_raw)],
+        axis=0,
+    )
+    filters = raw_weight * jnp.concatenate([info[:, :cycles] for info in by_pair], axis=0)
+    pair_sums[:group, :] = jnp.dot(
+        own_raw, own_framed[...], preferred_element_type=jnp.float32
+    )
+    pair_sums[group:, :] = jnp.dot(
+        other_raw, other_framed[...], preferred_element_type=jnp.float32
+    )
     share_part.wait()
     theirs = part_recv[...]
     theirs = jnp.concatenate([theirs[part_dev:, :], theirs[:part_dev, :]], axis=0)
@@ -362,34 +380,17 @@
     evidence_row = jnp.sum(jnp.where(corner, evidence, 0.0), axis=0, keepdims=True)
     evidence_ref[...] = evidence_row[:, :part_dev]
 
-    def posteriors(found, evidence):
-        parts = [jnp.where(live, jnp.exp(value - evidence), 0.0) for live, value in found]
-        return jnp.concatenate(parts, axis=0).astype(jnp.bfloat16)
-
-    own_post = posteriors(own_found, evidence[:part_dev])
-    other_post = posteriors(other_found, evidence[part_dev:])
-    weight = jnp.concatenate(
-        [
-            jnp.sum(post.astype(jnp.float32), axis=1, keepdims=True)
-            for post in (own_post, other_post)
-        ],
-        axis=0,
-    )
-    filters = weight * jnp.concatenate([info[:, :cycles] for info in by_pair], axis=0)
+    scale = jnp.exp(peak - evidence)
+    scale = jnp.concatenate([scale[:part_dev]] * 2 + [scale[part_dev:]] * 2, axis=0)
+    filters = filters * scale
 
     chips = doms // 2
     chip, core = me // 2, lax.rem(me, 2)
     copies = []
-    for step in sorted(range(chips), key=lambda step: -min(step, chips - step)):
+    for step in [*range(1, chips), 0]:
         target = lax.rem(chip + step, chips)
         lanes = pl.ds(pl.multiple_of(target * 2 * share, LANES), 2 * share)
-        terms = jnp.concatenate(
-            [
-                jnp.dot(own_post, own_framed[:, lanes], preferred_element_type=jnp.float32),
-                jnp.dot(other_post, other_framed[:, lanes], preferred_element_type=jnp.float32),
-            ],
-            axis=0,
-        )
+        terms = pair_sums[:, lanes] * scale
         for to in range(2):
             here = pl.ds(pl.multiple_of((2 * target + to) * pairs, pairs), pairs)
             stage[here, :] = jnp.concatenate(
@@ -486,6 +487,7 @@
             pltpu.VMEM((pairs, LANES), bf16),
             pltpu.VMEM((doms * pairs, LANES), bf16),
             pltpu.VMEM((doms * pairs, wide), bf16),
+            pltpu.VMEM((pairs, features), f32),
             pltpu.SemaphoreType.DMA((5,)),
             pltpu.SemaphoreType.DMA((2,)),
             pltpu.SemaphoreType.DMA((2,)),

time: 26.9 us -> 25 us (0.929); the launches traced: 26.4 us -> 24.8 us
  Pallas kernels: 25.8 us -> 24.2 us
    pallas_call x1, Pallas kernels: 23.7 us -> 22.1 us  [paired_shards(): pl.pallas_call(functools.partial(estep_kernel, doms), out_shape=(jax.Shap...]
where the time goes in v5:
time: 25 us; the launch traced here: 24.8 us
  Pallas kernels  24.2 us (97%)
  between operations  0.64 us (3%)
    pallas_call x1, Pallas kernels, paired_shards(): pl.pallas_call(functools.partial(estep_kernel, doms), out_shape=(jax.Shap...  22.1 us
    pallas_call x1, Pallas kernels, paired_shards(): pl.pallas_call(sums_kernel, out_shape=(jax.ShapeDtypeStruct((class_block,...  2.14 us

profile of v5, /device:TPU:1, one launch (start us, length us, event | category | flops | bytes accessed | tf_op | source)
XLA Modules:
  0.0 24.8 jit_solution(14358324690442269236)
XLA Ops:
  0.6 22.1 %shard_map.76 = (bf16[256,640]{1,0:T(8,128)(2,1)}, bf16[256,200]{1,0:T(8,128)(2,1)}, f32[1,4]{1,0:T(1,128)}) custom-call(bf16[4,9216]{1,0:T(4,128)(2,1)} %images_ref.1, f32[4,64]{1,0:T(4,128)} %ctf_ref.1, f32[1,64]{1,0:T(1,128)} %bitcast.6, s32[2,4]{1,0:T(2,128)} %bitcast.5, bf16[200,9216]{1,0:T(8,128)(2,1)} %classes_ref.1), custom_call_target="tpu_custom_call" | custom-call | tf_op jit(solution)/shard_map/pallas_call | solution.py:464
  22.7 2.1 %shard_map.77 = (f32[200,576]{1,0:T(8,128)}, f32[64,200]{1,0:T(8,128)}, f32[1,4]{1,0:T(1,128)}) custom-call(bf16[256,640]{1,0:T(8,128)(2,1)} %get-tuple-element.9.arrived, bf16[256,200]{1,0:T(8,128)(2,1)} %get-tuple-element.10.chosen, f32[1,4]{1,0:T(1,128)} %get-tuple-element.11.evidence_in), custom_call_target="tpu_custom_call" | custom-call | tf_op jit(solution)/shard_map/pallas_call | solution.py:503

commit v6 on v5

--- a/solution.py
+++ b/solution.py
@@ -159,7 +159,6 @@
     cand_ref,
     classes_ref,
     arrived,
-    chosen_ref,
     evidence_ref,
     held,
     images_vmem,
@@ -174,15 +173,11 @@
     other_framed,
     part_send,
     part_recv,
-    ids_send,
-    ids_recv,
     stage,
     pair_sums,
     load_sem,
     pair_send_sem,
     pair_recv_sem,
-    ids_send_sem,
-    ids_recv_sem,
     data_send_sem,
     data_recv_sem,
 ):
@@ -325,7 +320,7 @@
     )
     share_part.start()
     by_pair = [own_info, own_info, other_info, other_info]
-    ids_send[...] = jnp.concatenate(
+    pair_ids = jnp.concatenate(
         [
             jnp.broadcast_to(
                 info[:, (2 + place % 2) * cycles : (2 + place % 2) * cycles + 1], (part_dev, LANES)
@@ -333,22 +328,8 @@
             for place, info in enumerate(by_pair)
         ],
         axis=0,
-    ).astype(jnp.bfloat16)
+    )
     mine = pl.ds(pl.multiple_of(me * pairs, pairs), pairs)
-    ids_recv[mine, :] = ids_send[...]
-    id_copies = []
-    for step, peer in enumerate(peers):
-        copy = pltpu.make_async_remote_copy(
-            src_ref=ids_send,
-            dst_ref=ids_recv.at[mine, :],
-            send_sem=ids_send_sem.at[step],
-            recv_sem=ids_recv_sem.at[step],
-            device_id={"dom": peer},
-            device_id_type=MESH,
-        )
-        copy.start()
-        id_copies.append(copy)
-
     def raw_weights(found, peak):
         parts = [jnp.where(live, jnp.exp(value - peak), 0.0) for live, value in found]
         return jnp.concatenate(parts, axis=0).astype(jnp.bfloat16)
@@ -394,7 +375,7 @@
         for to in range(2):
             here = pl.ds(pl.multiple_of((2 * target + to) * pairs, pairs), pairs)
             stage[here, :] = jnp.concatenate(
-                [terms[:, to * share : (to + 1) * share], filters], axis=1
+                [terms[:, to * share : (to + 1) * share], filters, pair_ids], axis=1
             ).astype(jnp.bfloat16)
         for to in range(2 if step else 1):
             peer = 2 * target + to if step else me + 1 - 2 * core
@@ -410,13 +391,6 @@
             copies.append((copy, 2 * step + to, peer))
     arrived[mine, :] = stage[mine, :]
 
-    for copy in id_copies:
-        copy.wait()
-    ids = jnp.broadcast_to(
-        ids_recv[...].astype(jnp.float32)[:, :1], (doms * pairs, class_block)
-    )
-    column = lax.broadcasted_iota(jnp.int32, (doms * pairs, class_block), 1).astype(jnp.float32)
-    chosen_ref[...] = jnp.where(ids == column, 1.0, 0.0).astype(jnp.bfloat16)
     for copy, place, peer in copies:
         copy.wait_send()
         pltpu.make_async_remote_copy(
@@ -429,18 +403,22 @@
         ).wait_recv()
 
 
-def sums_kernel(arrived, chosen, evidence_in, sums_ref, weight_ref, evidence_ref):
+def sums_kernel(arrived, evidence_in, sums_ref, weight_ref, evidence_ref):
     share = sums_ref.shape[1]
     cycles = weight_ref.shape[0]
     contract_first = (((0,), (0,)), ((), ()))
     evidence_ref[...] = evidence_in[...]
+    block = (arrived.shape[0], sums_ref.shape[0])
+    ids = arrived[:, share + cycles :].astype(jnp.float32)[:, :1]
+    column = lax.broadcasted_iota(jnp.int32, block, 1).astype(jnp.float32)
+    chosen = jnp.where(jnp.broadcast_to(ids, block) == column, 1.0, 0.0).astype(jnp.bfloat16)
     sums = lax.dot_general(
-        chosen[...], arrived[...], contract_first, preferred_element_type=jnp.float32
+        chosen, arrived[:, : share + cycles], contract_first, preferred_element_type=jnp.float32
     )
     sums_ref[...] = sums[:, :share]
     filter_sums = lax.dot_general(
-        arrived[:, share - cycles :],
-        chosen[...],
+        arrived[:, share - cycles : share + cycles],
+        chosen,
         contract_first,
         preferred_element_type=jnp.float32,
     )
@@ -457,19 +435,18 @@
     rows = ROTATIONS * part_dev
     pairs = TOP_CAND * group
     share = features // doms
-    wide = share + cycles
+    wide = share + cycles + LANES
     own_rows = rows + 16
     f32, bf16 = jnp.float32, jnp.bfloat16
     vmem = pl.BlockSpec(memory_space=pltpu.VMEM)
-    arrived, chosen, evidence = pl.pallas_call(
+    arrived, evidence = pl.pallas_call(
         functools.partial(estep_kernel, doms),
         out_shape=(
             jax.ShapeDtypeStruct((doms * pairs, wide), bf16),
-            jax.ShapeDtypeStruct((doms * pairs, class_block), bf16),
             jax.ShapeDtypeStruct((1, part_dev), f32),
         ),
         in_specs=[pl.BlockSpec(memory_space=pltpu.HBM)] * 5,
-        out_specs=(vmem, vmem, vmem),
+        out_specs=(vmem, vmem),
         scratch_shapes=[
             pltpu.VMEM((class_block, features), bf16),
             pltpu.VMEM((part_dev, features), bf16),
@@ -484,15 +461,11 @@
             pltpu.VMEM((rows, features), bf16),
             pltpu.VMEM((group, LANES), f32),
             pltpu.VMEM((group, LANES), f32),
-            pltpu.VMEM((pairs, LANES), bf16),
-            pltpu.VMEM((doms * pairs, LANES), bf16),
             pltpu.VMEM((doms * pairs, wide), bf16),
             pltpu.VMEM((pairs, features), f32),
             pltpu.SemaphoreType.DMA((5,)),
             pltpu.SemaphoreType.DMA((2,)),
             pltpu.SemaphoreType.DMA((2,)),
-            pltpu.SemaphoreType.DMA((doms - 1,)),
-            pltpu.SemaphoreType.DMA((doms - 1,)),
             pltpu.SemaphoreType.DMA((doms,)),
             pltpu.SemaphoreType.DMA((doms,)),
         ],
@@ -507,10 +480,10 @@
             jax.ShapeDtypeStruct((cycles, class_block), f32),
             jax.ShapeDtypeStruct((1, part_dev), f32),
         ),
-        in_specs=[vmem] * 3,
+        in_specs=[vmem] * 2,
         out_specs=(vmem, vmem, vmem),
         compiler_params=pltpu.CompilerParams(vmem_limit_bytes=63 * 1024 * 1024),
-    )(arrived, chosen, evidence)
+    )(arrived, evidence)
     return sums.T, weight.T, evidence.reshape(part_dev)
 
 

time: 25 us -> 25.7 us (1.028)
  Pallas kernels: 24.2 us -> 24.7 us
    pallas_call x1, Pallas kernels: 22.1 us -> 22.6 us  [paired_shards(): pl.pallas_call(functools.partial(estep_kernel, doms), out_shape=(jax.Shap...]
where the time goes in v6:
time: 25.7 us; the launch traced here: 25.4 us
  Pallas kernels  24.7 us (96%)
  between operations  0.64 us (2%)
    pallas_call x1, Pallas kernels, paired_shards(): pl.pallas_call(functools.partial(estep_kernel, doms), out_shape=(jax.Shap...  22.6 us
    pallas_call x1, Pallas kernels, paired_shards(): pl.pallas_call(sums_kernel, out_shape=(jax.ShapeDtypeStruct((class_block,...  2.18 us

profile of v6, /device:TPU:1, one launch (start us, length us, event | category | flops | bytes accessed | tf_op | source)
XLA Modules:
  0.0 25.4 jit_solution(4943995011802360545)
XLA Ops:
  0.6 22.6 %shard_map.76 = (bf16[256,768]{1,0:T(8,128)(2,1)}, f32[1,4]{1,0:T(1,128)}) custom-call(bf16[4,9216]{1,0:T(4,128)(2,1)} %images_ref.1, f32[4,64]{1,0:T(4,128)} %ctf_ref.1, f32[1,64]{1,0:T(1,128)} %bitcast.6, s32[2,4]{1,0:T(2,128)} %bitcast.5, bf16[200,9216]{1,0:T(8,128)(2,1)} %classes_ref.1), custom_call_target="tpu_custom_call" | custom-call | tf_op jit(solution)/shard_map/pallas_call | solution.py:442
  23.2 2.2 %shard_map.77 = (f32[200,576]{1,0:T(8,128)}, f32[64,200]{1,0:T(8,128)}, f32[1,4]{1,0:T(1,128)}) custom-call(bf16[256,768]{1,0:T(8,128)(2,1)} %get-tuple-element.8.arrived, f32[1,4]{1,0:T(1,128)} %get-tuple-element.9.evidence_in), custom_call_target="tpu_custom_call" | custom-call | tf_op jit(solution)/shard_map/pallas_call | solution.py:476

commit v7 on v5

--- a/solution.py
+++ b/solution.py
@@ -387,7 +387,8 @@
     chips = doms // 2
     chip, core = me // 2, lax.rem(me, 2)
     copies = []
-    for step in [*range(1, chips), 0]:
+    order = [1, chips // 2, *(step for step in range(2, chips) if step != chips // 2), 0]
+    for step in order:
         target = lax.rem(chip + step, chips)
         lanes = pl.ds(pl.multiple_of(target * 2 * share, LANES), 2 * share)
         terms = pair_sums[:, lanes] * scale

time: 25 us -> 25.9 us (1.036); the launches traced: 24.8 us -> 25.4 us
  Pallas kernels: 24.2 us -> 24.8 us
    pallas_call x1, Pallas kernels: 22.1 us -> 22.6 us  [paired_shards(): pl.pallas_call(functools.partial(estep_kernel, doms), out_shape=(jax.Shap...]
where the time goes in v7:
time: 25.9 us; the launch traced here: 25.4 us
  Pallas kernels  24.8 us (96%)
  between operations  0.64 us (2%)
    pallas_call x1, Pallas kernels, paired_shards(): pl.pallas_call(functools.partial(estep_kernel, doms), out_shape=(jax.Shap...  22.6 us
    pallas_call x1, Pallas kernels, paired_shards(): pl.pallas_call(sums_kernel, out_shape=(jax.ShapeDtypeStruct((class_block,...  2.14 us

profile of v7, /device:TPU:1, one launch (start us, length us, event | category | flops | bytes accessed | tf_op | source)
XLA Modules:
  0.0 25.4 jit_solution(17480927410533586172)
XLA Ops:
  0.6 22.6 %shard_map.76 = (bf16[256,640]{1,0:T(8,128)(2,1)}, bf16[256,200]{1,0:T(8,128)(2,1)}, f32[1,4]{1,0:T(1,128)}) custom-call(bf16[4,9216]{1,0:T(4,128)(2,1)} %images_ref.1, f32[4,64]{1,0:T(4,128)} %ctf_ref.1, f32[1,64]{1,0:T(1,128)} %bitcast.6, s32[2,4]{1,0:T(2,128)} %bitcast.5, bf16[200,9216]{1,0:T(8,128)(2,1)} %classes_ref.1), custom_call_target="tpu_custom_call" | custom-call | tf_op jit(solution)/shard_map/pallas_call | solution.py:465
  23.3 2.1 %shard_map.77 = (f32[200,576]{1,0:T(8,128)}, f32[64,200]{1,0:T(8,128)}, f32[1,4]{1,0:T(1,128)}) custom-call(bf16[256,640]{1,0:T(8,128)(2,1)} %get-tuple-element.9.arrived, bf16[256,200]{1,0:T(8,128)(2,1)} %get-tuple-element.10.chosen, f32[1,4]{1,0:T(1,128)} %get-tuple-element.11.evidence_in), custom_call_target="tpu_custom_call" | custom-call | tf_op jit(solution)/shard_map/pallas_call | solution.py:504
